TPU v7x, 32 devices: a whole 2x2x4 slice. The times are simulated.
32 devices in a mesh: grp: 2 (over y), chan: 2 (over x), tm: 4 (over z), pol: 2 (over core).
Axes of the slice: x: 2, y: 2, z: 4, core: 2. Of those that a mesh axis runs over, the one named last changes fastest.
Arguments:
- voltages: bfloat16 [4, 2, 256, 32768], P('grp', 'pol', 'chan', 'tm'), parts along dimension 0, may hold values from -6 to 6
- taps_filter: float32 [16, 2048], replicated, may hold values from -1.5 to 1.5
- tile_a: int32 [14, 64], replicated, may hold values from 0 to 255
- tile_b: int32 [14, 64], replicated, may hold values from 0 to 255
- tile_owner: int32 [14], replicated, may hold values from 0 to 1, as said below
- tile_flags: int32 [14, 16], replicated, may hold values 0 or 1
Outputs:
- visibility: float32 [16, 256, 4, 2, 64, 128], P('pol', ('chan', 'tm'), 'grp'), parts along dimension 2
There are 2 independent parts, one for each index of `grp`. A program takes and returns all parts, laid end to end along the dimension named above; an argument that names none is the same for every part. Nothing has to cross between parts.
Inputs may be any that keep to these rules, and one draw needn't show every extreme that they name: `tile_owner`: one owner holds exactly 8 tiles and the other owner holds all the rest.
All inputs are finite; a program needn't handle non-finite values.
Results may differ from a plain program's by a relative error of at most 0.0035.
Values may be sent and summed in bfloat16 or wider, within the bound.
No kernel may reach another device: no remote copies, remote signals or barrier semaphores. Data moves between devices by JAX's collectives and lax.ppermute only.
A program may use at most 128 MiB of HBM per device.

v0:
```python
import math

import jax
import jax.numpy as jnp
import numpy as np
from jax import lax
from jax.experimental import pallas as pl
from jax.experimental.pallas import tpu as pltpu
from jax.sharding import PartitionSpec as P

AVG = 8
CAP = 8
RADIX = 16
LANES = 128
ROWS = 16


radix_first = 32


def from_behind(value, axis, steps):
    count = lax.axis_size(axis)
    first, last = (max(0, -steps), min(count, count - steps))
    return lax.ppermute(value, axis, [(source, source + steps) for source in range(first, last)])


def fourier(filtered):
    length = filtered.shape[-1]
    second = length // radix_first
    exact_mode = lax.Precision.HIGHEST
    grid = filtered.reshape(filtered.shape[:-1] + (radix_first, second))
    outer = jnp.arange(radix_first, dtype=jnp.int32)
    inner = jnp.arange(second, dtype=jnp.int32)
    phase_one = (
        2.0
        * math.pi
        / radix_first
        * (outer[:, None] * outer[None, :] % radix_first).astype(jnp.float32)
    )
    phase_twist = 2.0 * math.pi / length * (outer[:, None] * inner[None, :]).astype(jnp.float32)
    phase_two = (
        2.0 * math.pi / second * (inner[:, None] * inner[None, :] % second).astype(jnp.float32)
    )
    cos_one, sin_one = (jnp.cos(phase_one), jnp.sin(phase_one))
    cos_twist, sin_twist = (jnp.cos(phase_twist), jnp.sin(phase_twist))
    cos_two, sin_two = (jnp.cos(phase_two), jnp.sin(phase_two))
    first_form = "fk,stkj->stfj"
    section_re = jnp.einsum(first_form, cos_one, grid[0], precision=exact_mode) + jnp.einsum(
        first_form, sin_one, grid[1], precision=exact_mode
    )
    section_im = jnp.einsum(first_form, cos_one, grid[1], precision=exact_mode) - jnp.einsum(
        first_form, sin_one, grid[0], precision=exact_mode
    )
    turned_re = section_re * cos_twist + section_im * sin_twist
    turned_im = section_im * cos_twist - section_re * sin_twist
    second_form = "gj,stfj->stgf"
    final_re = jnp.einsum(second_form, cos_two, turned_re, precision=exact_mode) + jnp.einsum(
        second_form, sin_two, turned_im, precision=exact_mode
    )
    final_im = jnp.einsum(second_form, cos_two, turned_im, precision=exact_mode) - jnp.einsum(
        second_form, sin_two, turned_re, precision=exact_mode
    )
    joined = jnp.stack([final_re, final_im]).reshape(filtered.shape)
    return joined * (1.0 / math.sqrt(length))


def correlate(full, rows_a, rows_b, flags, group_count):
    depth = full.shape[4]
    weight = jnp.tile(flags.astype(jnp.bfloat16), depth // flags.shape[0])
    left_rows = jnp.take(full, rows_a, axis=2) * weight
    right_rows = jnp.take(full, rows_b, axis=2)
    stacked_left = jnp.stack(
        [
            jnp.concatenate([left_rows[0], left_rows[1]], axis=-1),
            jnp.concatenate([left_rows[1], -left_rows[0]], axis=-1),
        ]
    )
    joined_right = jnp.concatenate([right_rows[0], right_rows[1]], axis=-1)
    result = jnp.einsum(
        "rpank,qbnk->nrpaqb", stacked_left, joined_right, preferred_element_type=jnp.float32
    )
    width = rows_a.shape[0]
    return result.reshape(group_count, 2, 2, width, 2 * width) * (1.0 / depth)


def on_device_any(voltages, taps_filter, tile_a, tile_b, tile_owner, tile_flags):
    history = taps_filter.shape[0] - 1
    length = taps_filter.shape[1]
    stations = voltages.shape[2]
    frames = voltages.shape[3] // length
    local_blocks = voltages.reshape(2, stations, frames, length)
    hop_count = -(-history // frames)
    sending = local_blocks
    extended = local_blocks
    for hop_index in range(hop_count):
        sending = from_behind(sending, "tm", 1)
        extended = jnp.concatenate([sending, extended], axis=2)
    extended = extended[:, :, extended.shape[2] - history - frames :]
    filtered = jnp.zeros((2, stations, frames, length), jnp.float32)
    for tap_index in range(history + 1):
        start = history - tap_index
        filtered = filtered + taps_filter[tap_index] * extended[
            :, :, start : start + frames
        ].astype(jnp.float32)
    spectra = fourier(filtered).astype(jnp.bfloat16)
    chan_count = lax.axis_size("chan")
    time_count = lax.axis_size("tm")
    narrow = length // (chan_count * time_count)
    outgoing = spectra.reshape(2, stations, frames, chan_count, time_count, narrow)
    outgoing = outgoing.transpose(0, 3, 4, 5, 1, 2)
    flat = outgoing.reshape(2, chan_count * time_count, narrow, stations * frames)
    moved = lax.all_to_all(flat, ("chan", "tm"), split_axis=1, concat_axis=1, tiled=True)
    moved = moved.reshape(2, chan_count, time_count, narrow, stations, frames)
    bands = narrow // AVG
    every_station = chan_count * stations
    spectra_count = time_count * frames
    arranged = moved.transpose(0, 1, 4, 3, 2, 5).reshape(
        2, 1, every_station, bands, AVG * spectra_count
    )
    full = lax.all_gather(arranged, "pol", axis=1, tiled=True)
    position = lax.axis_index("pol")
    width = tile_a.shape[1]
    capacity = CAP
    held = tile_owner == position
    listed = jnp.nonzero(held, size=capacity, fill_value=0)[0].astype(jnp.int32)
    tally = jnp.sum(held.astype(jnp.int32))
    initial = jnp.zeros((capacity, bands, 2, 2, width, 2 * width), jnp.float32)

    def fill_slot(slot, results):
        chosen_tile = listed[slot]
        return results.at[slot].set(
            correlate(
                full, tile_a[chosen_tile], tile_b[chosen_tile], tile_flags[chosen_tile], bands
            )
        )

    visibility = lax.fori_loop(0, tally, fill_slot, initial)
    return visibility


def fourier_tables(length):
    low = np.arange(RADIX)
    lane = np.arange(LANES)
    turn = 2.0 * np.pi / length * np.outer(low, lane)
    twiddle = np.stack([np.cos(turn), np.sin(turn)]).astype(np.float32)
    angle = 2.0 * np.pi / LANES * (np.outer(lane, lane) % LANES)
    cos, sin = np.cos(angle) / math.sqrt(length), np.sin(angle) / math.sqrt(length)
    matrix = np.block([[cos, sin], [-sin, cos]]).astype(np.float32)
    high = matrix.astype(jnp.bfloat16)
    rest = (matrix - high.astype(np.float32)).astype(jnp.bfloat16)
    return twiddle, np.stack([high, rest])


def butterflies(values):
    count = len(values)
    if count == 1:
        return values
    even, odd = butterflies(values[0::2]), butterflies(values[1::2])
    first, second = [], []
    for index in range(count // 2):
        (a, b), (c, d) = even[index], odd[index]
        if index == 0:
            e, f = c, d
        elif 4 * index == count:
            e, f = d, -c
        elif 8 * index == count:
            root = math.sqrt(0.5)
            e, f = (c + d) * root, (d - c) * root
        elif 8 * index == 3 * count:
            root = math.sqrt(0.5)
            e, f = (d - c) * root, -(c + d) * root
        else:
            turn = 2.0 * math.pi * index / count
            cos, sin = math.cos(turn), math.sin(turn)
            e, f = c * cos + d * sin, d * cos - c * sin
        first.append((a + e, b + f))
        second.append((a - e, b - f))
    return first + second


def channelise_kernel(frames, chunk, columns, plan, place_ref, own_ref, *refs):
    sources = refs[-6].shape[0]
    come_refs = refs[: sources - 1]
    taps_ref, twiddle_ref, matrix_ref = refs[sources - 1 : sources + 2]
    out_refs = refs[sources + 2 : -6]
    x_ref, fil_ref, zr_ref, zi_ref, w_ref, sems = refs[-6:]
    chan, tm = place_ref[0], place_ref[1]
    own_rows = pl.multiple_of((tm * (own_ref.shape[1] // (sources * ROWS)) + chunk) * ROWS, ROWS)
    copies = []
    for behind in range(sources):
        block = come_refs[behind - 1] if behind else own_ref.at[:, pl.ds(own_rows, ROWS), :]
        slot = lax.rem(tm - behind + sources, sources)
        copies.append(pltpu.make_async_copy(block, x_ref.at[slot], sems.at[behind]))
    for copy in copies:
        copy.start()
    for copy in copies:
        copy.wait()
    spectra = sources * frames
    length = taps_ref.shape[1]
    taps = taps_ref.shape[0]
    depth = RADIX * spectra
    z_refs = (zr_ref, zi_ref)

    @pl.loop(0, RADIX)
    def _(section):
        at = pl.multiple_of(section * LANES, LANES)
        weights = [taps_ref[pl.ds(m, 1), pl.ds(at, LANES)] for m in range(taps)]
        for part in range(2):
            blocks = []
            for t in range(spectra):
                lane = pl.multiple_of((t % frames) * length + section * LANES, LANES)
                blocks.append(x_ref[t // frames, part, :, pl.ds(lane, LANES)].astype(jnp.float32))
            for t in range(spectra):
                total = weights[0] * blocks[t]
                for m in range(1, min(t + 1, taps)):
                    total = total + weights[m] * blocks[t - m]
                fil_ref[section, t, part] = total

    @pl.loop(0, spectra)
    def _(t):
        for half in range(ROWS // 8):
            values = [
                tuple(fil_ref[section, t, part, pl.ds(half * 8, 8), :] for part in range(2))
                for section in range(RADIX)
            ]
            for low, (re, im) in enumerate(butterflies(values)):
                if low:
                    cos = twiddle_ref[0, pl.ds(low, 1), :]
                    sin = twiddle_ref[1, pl.ds(low, 1), :]
                    re, im = re * cos + im * sin, im * cos - re * sin
                rows = pl.ds(half * 8 * depth + low * spectra + t, 8, stride=depth)
                zr_ref[rows, :] = re
                zi_ref[rows, :] = im

    form = (((1,), (1,)), ((), ()))
    high_matrix, low_matrix = matrix_ref[0], matrix_ref[1]
    halves = depth // LANES

    @pl.loop(0, ROWS)
    def _(station):
        rows = pl.ds(pl.multiple_of(station * depth, depth), depth)
        value = jnp.concatenate([ref[rows, :] for ref in z_refs], axis=1)
        high = value.astype(jnp.bfloat16)
        rest = (value - high.astype(jnp.float32)).astype(jnp.bfloat16)
        total = lax.dot_general(high_matrix, high, form, preferred_element_type=jnp.float32)
        total += lax.dot_general(high_matrix, rest, form, preferred_element_type=jnp.float32)
        total += lax.dot_general(low_matrix, high, form, preferred_element_type=jnp.float32)
        for half in range(halves):
            for part in range(2):
                rows = pl.ds((half * 2 + part) * ROWS + station, LANES, stride=halves * 2 * ROWS)
                w_ref[rows, :] = total[
                    part * LANES : (part + 1) * LANES, half * LANES : (half + 1) * LANES
                ]

    share = w_ref.shape[0] // (columns * sources)
    band_rows = 2 * ROWS
    piece = 4 * band_rows
    for blocks, out_ref in zip(plan, out_refs):
        at = 0
        for across, along, start, stop in blocks:
            owner = lax.rem(chan + across, columns) * sources + lax.rem(tm + along, sources)
            for row in range(start * band_rows, stop * band_rows, piece):
                rows = pl.ds(pl.multiple_of(owner * share + row, piece), piece)
                out_ref[at : at + piece, :] = w_ref[rows, :].astype(jnp.bfloat16)
                at += piece


def channelise(place, chunk, voltages, come, taps_filter, tables, frames, columns, plan):
    sources = 1 + len(come)
    length = taps_filter.shape[1]
    spectra = sources * frames
    twiddle, matrix = tables
    out_rows = length // AVG * 2 * ROWS
    whole = pl.BlockSpec(memory_space=pltpu.VMEM)
    counts = [sum(stop - start for _, _, start, stop in blocks) for blocks in plan]
    flat = pl.pallas_call(
        lambda *refs: channelise_kernel(frames, chunk, columns, plan, *refs),
        out_shape=[
            jax.ShapeDtypeStruct((count * 2 * ROWS, LANES), jnp.bfloat16) for count in counts
        ],
        in_specs=[pl.BlockSpec(memory_space=pltpu.SMEM)]
        + [pl.BlockSpec(memory_space=pl.ANY)] * sources
        + [whole] * 3,
        out_specs=[whole] * len(plan),
        scratch_shapes=[
            pltpu.VMEM((sources, 2, ROWS, frames * length), jnp.bfloat16),
            pltpu.VMEM((RADIX, spectra, 2, ROWS, LANES), jnp.float32),
            pltpu.VMEM((ROWS * RADIX * spectra, LANES), jnp.float32),
            pltpu.VMEM((ROWS * RADIX * spectra, LANES), jnp.float32),
            pltpu.VMEM((out_rows, LANES), jnp.float32),
            pltpu.SemaphoreType.DMA((sources,)),
        ],
        compiler_params=pltpu.CompilerParams(vmem_limit_bytes=40 * 2**20),
        cost_estimate=pl.CostEstimate(
            flops=9 * 10**9, bytes_accessed=4 * 2**20, transcendentals=0
        ),
        name="channelise",
    )(place, voltages, *come, taps_filter, jnp.asarray(twiddle), jnp.asarray(matrix))
    return [piece.reshape(count, 2, ROWS, LANES) for piece, count in zip(flat, counts)]


def correlate_kernel(starts, width, place_ref, left_sel_ref, right_sel_ref, weight_ref, *refs):
    x_refs, (out_ref, x_all, *rows_refs, sems) = refs[: 2 * len(starts)], refs[-7:]
    tiles = out_ref.shape[0]
    step = pl.program_id(0)
    bands = x_all.shape[2]
    spans = [(0, 2), (2, bands)]

    def copies(span):
        first, last = spans[span]
        block = 0
        for index, start in enumerate(starts):
            blocks = x_refs[2 * index].shape[0]
            for side in range(2):
                yield pltpu.make_async_copy(
                    x_refs[2 * index + side].at[:, pl.ds(start + first, last - first)],
                    x_all.at[
                        lax.rem(place_ref[2] + side, 2),
                        pl.ds(block, blocks),
                        pl.ds(first, last - first),
                    ],
                    sems.at[span, 2 * index + side],
                )
            block += blocks

    lower = lax.broadcasted_iota(jnp.int32, (1, 2 * width), 1) < width

    def gather(band, left_ref, right_ref):
        right = []
        for pol in range(2):
            lanes = slice(pol * 2 * LANES, (pol + 1) * 2 * LANES)
            value = jnp.concatenate(
                [
                    jnp.concatenate([x_all[pol, block, band, part] for part in range(2)], axis=1)
                    for block in range(x_all.shape[1])
                ]
            )
            left = jnp.dot(left_sel_ref[...], value, preferred_element_type=jnp.float32)
            for tile in range(tiles):
                rows = slice(tile * width, (tile + 1) * width)
                scaled = left[rows] * weight_ref[pl.ds(tile, 1), :]
                left_ref[rows, lanes] = scaled.astype(jnp.bfloat16)
            right.append(
                lax.dot_general(
                    value,
                    right_sel_ref[pol],
                    (((0,), (0,)), ((), ())),
                    preferred_element_type=jnp.float32,
                )
            )
        for pair in range(tiles // 2):
            first, second = (v[:, pair * 2 * width : (pair + 1) * 2 * width] for v in right)
            even = jnp.where(lower, first, second)
            odd = pltpu.roll(jnp.where(lower, second, first), width, 1)
            right_ref[2 * pair] = even.astype(jnp.bfloat16)
            right_ref[2 * pair + 1] = odd.astype(jnp.bfloat16)

    def multiply(number, left_ref, right_ref):
        for tile in range(tiles):
            rows = slice(tile * width, (tile + 1) * width)
            left = jnp.concatenate(
                [left_ref[rows, lanes : lanes + 2 * LANES] for lanes in (0, 2 * LANES)]
            )
            right = right_ref[tile]
            turned = jnp.concatenate([-right[LANES:], right[:LANES]])
            both = jnp.concatenate([right, turned], axis=1)
            result = jnp.dot(left, both, preferred_element_type=jnp.float32)
            for part in range(2):
                out_ref[tile, number, part] = result[
                    :, part * 2 * width : (part + 1) * 2 * width
                ].reshape(2, width, 2 * width)

    even, odd = rows_refs[:2], rows_refs[2:]

    @pl.when(step == 0)
    def _():
        for span in range(2):
            for copy in copies(span):
                copy.start()
        for copy in copies(0):
            copy.wait()
        gather(0, *even)
        for copy in copies(1):
            copy.wait()

    gather(2 * step + 1, *odd)
    multiply(0, *even)
    gather(jnp.minimum(2 * step + 2, bands - 1), *even)
    multiply(1, *odd)


def correlate_tiles(place, tables, pieces, starts, width, first, count, bands, earlier):
    left_select, _, weight = tables
    tiles = weight.shape[0]
    whole = pl.BlockSpec(memory_space=pltpu.VMEM)
    more = [] if earlier is None else [earlier]
    rows = [
        pltpu.VMEM((tiles * width, 4 * LANES), jnp.bfloat16),
        pltpu.VMEM((tiles, 2 * LANES, 2 * width), jnp.bfloat16),
    ]
    return pl.pallas_call(
        lambda *refs: correlate_kernel(starts, width, *refs),
        grid=(count // 2,),
        out_shape=jax.ShapeDtypeStruct((tiles, bands, 2, 2, width, 2 * width), jnp.float32),
        in_specs=[pl.BlockSpec(memory_space=pltpu.SMEM)]
        + [whole] * len(tables)
        + [pl.BlockSpec(memory_space=pl.ANY)] * (len(pieces) + len(more)),
        out_specs=pl.BlockSpec(
            (tiles, 2, 2, 2, width, 2 * width), lambda g: (0, g + first // 2, 0, 0, 0, 0)
        ),
        scratch_shapes=[
            pltpu.VMEM((2, left_select.shape[1] // ROWS, count, 2, ROWS, LANES), jnp.bfloat16),
            *rows,
            *rows,
            pltpu.SemaphoreType.DMA((2, len(pieces))),
        ],
        input_output_aliases={1 + len(tables) + len(pieces): 0} if more else {},
        compiler_params=pltpu.CompilerParams(vmem_limit_bytes=32 * 2**20),
        cost_estimate=pl.CostEstimate(
            flops=13 * 10**9 * count // bands,
            bytes_accessed=42 * 2**20 * count // bands,
            transcendentals=0,
        ),
        name="correlate",
    )(place, *tables, *pieces, *more)


def tile_tables(tile_a, tile_b, tile_owner, tile_flags, row_of):
    tiles = tile_owner.shape[0]
    held = tile_owner == lax.axis_index("pol")
    order = jnp.arange(tiles, dtype=jnp.int32)
    rank = jnp.sum((held[None, :] & (order[None, :] < order[:, None])).astype(jnp.int32), axis=1)
    slots = jnp.arange(CAP, dtype=jnp.int32)
    pick = (held[None, :] & (rank[None, :] == slots[:, None])).astype(jnp.int32)
    sides = jnp.stack([row_of(tile_a), row_of(tile_b)], axis=1) + 1
    rows = jnp.sum(pick[:, :, None, None] * sides[None], axis=1) - 1
    flags = jnp.sum(pick[:, :, None] * tile_flags[None], axis=1).astype(jnp.float32)
    return rows, flags


def on_device_chunks(voltages, taps_filter, tile_a, tile_b, tile_owner, tile_flags):
    length = taps_filter.shape[1]
    stations = voltages.shape[2]
    frames = voltages.shape[3] // length
    chan_count, time_count = lax.axis_size("chan"), lax.axis_size("tm")
    owners = chan_count * time_count
    chunk_count = stations // (time_count * ROWS)
    width = tile_a.shape[1]
    bands = length // AVG // owners
    tables = fourier_tables(length)

    chan, tm = lax.axis_index("chan"), lax.axis_index("tm")
    place = jnp.stack([chan, tm, lax.axis_index("pol")]).astype(jnp.int32)

    def row_of(station):
        column, rest = station // stations, station % stations
        block, inside = rest // (chunk_count * ROWS), rest % (chunk_count * ROWS)
        across = (chan - column) % chan_count
        behind = (tm - block) % time_count
        piece = behind * chan_count + across
        return ((inside // ROWS) * owners + piece) * ROWS + inside % ROWS

    rows, flags = tile_tables(tile_a, tile_b, tile_owner, tile_flags, row_of)
    total_rows = chunk_count * owners * ROWS
    station_rows = jnp.arange(total_rows, dtype=jnp.int32)
    left_rows = rows[:, 0].reshape(-1)
    left_select = (left_rows[:, None] == station_rows).astype(jnp.bfloat16)
    right_rows = rows[:, 1].reshape(CAP // 2, 2, width)
    right_rows = jnp.stack([right_rows, right_rows[:, ::-1]]).reshape(2, 1, -1)
    right_select = (right_rows == station_rows[:, None]).astype(jnp.bfloat16)
    depth = AVG * time_count * frames
    weight = jnp.tile(flags * (1.0 / depth), (1, 2 * AVG))
    tables_of_tiles = [left_select, right_select, weight]

    samples = voltages.reshape(2, stations, frames * length)

    def travel(value, axes, distances):
        sizes = [lax.axis_size(axis) for axis in axes]
        pairs = []
        for index in np.ndindex(*sizes):
            target = [(i + d) % n for i, d, n in zip(index, distances, sizes)]
            pairs.append(tuple(int(np.ravel_multi_index(x, sizes)) for x in (index, target)))
        return lax.ppermute(value, axes, pairs)

    def after(values, earlier):
        return lax.optimization_barrier((list(values), list(earlier)))

    def block_for(values, chunk, distance):
        first = ((tm + distance) % time_count * chunk_count + chunk) * ROWS
        return lax.dynamic_slice(values, (0, first, 0), (2, ROWS, frames * length))

    def filtered(chunk, arrived, plan):
        return channelise(
            place, chunk, samples, arrived, taps_filter, tables, frames, chan_count, plan
        )

    def over(value, across, along):
        return travel(value, ("chan", "tm"), (across, along))

    def columns(near, far):
        return jnp.stack([near, far])

    cut = bands * 5 // 8
    rest = bands - cut
    pairs = [(x, z) for z in range(time_count) for x in range(chan_count)]
    early_pairs = [(x, z) for z in (1, 3) for x in range(2)]
    late_pairs = [(0, 2), (1, 2), (1, 0)]

    (one,), (values,) = after([block_for(samples, 0, 1)], [samples])
    two, three = (block_for(values, 0, distance) for distance in (2, 3))
    one, two = over(one, 0, 1), over(two, 0, 2)
    (three,), (one,) = after([three], [one])
    three = over(three, 0, 3)
    blocks = [block_for(values, 1, distance) for distance in (1, 2, 3)]
    blocks[:1], (two,) = after(blocks[:1], [two])
    blocks[2:], (three,) = after(blocks[2:], [three])
    first = [one, two, three]
    one, three = over(blocks[0], 0, 1), over(blocks[2], 0, 3)
    (two,), (one,) = after(blocks[1:2], [one])
    second = [one, over(two, 0, 2), three]

    plan = [[(x, z, 0, bands)] for x, z in pairs]
    early = dict(zip(pairs, filtered(0, first, plan)))
    blocks, held = after([early[p] for p in early_pairs], [second[1], *tables_of_tiles])
    second[1], tables_of_tiles = held[0], held[1:]
    early.update((p, over(block, *p)) for p, block in zip(early_pairs, blocks))
    spans = [(0, cut), (cut, bands)]
    hops = [1, 2, 3]
    plan = [[(0, z, *span) for span in spans for z in range(time_count)]]
    plan += [[(1, z, *span) for span in spans for z in hops], [(1, 0, *span) for span in spans]]
    near, far, home = filtered(1, second, plan)
    blocks, (near,) = after([early[p] for p in late_pairs], [near])
    early.update((p, over(block, *p)) for p, block in zip(late_pairs, blocks))
    (far,), held = after([far], [early[p] for p in early_pairs[:4]])
    early.update(zip(early_pairs[:4], held))
    far = over(far, 1, 0)
    def mix(start, index, other_start, other, count):
        first, second = start + index * count, other_start + index * count
        return columns(near[first : first + count], other[second : second + count])

    blocks = {z: mix(0, z, -cut, far, cut) for z in hops}
    (blocks[1], blocks[3]), held = after([blocks[1], blocks[3]], [early[p] for p in late_pairs[:1]])
    early.update(zip(late_pairs[:1], held))
    one, three = over(blocks[1], 0, 1), over(blocks[3], 0, 3)
    (block,), (one,) = after([blocks[2]], [one])
    two = over(block, 0, 2)
    (home,), (three,) = after([home], [three])
    home = over(home, 1, 0)
    low = [mix(0, 0, 0, home, cut), one, two, three]
    high = [mix(time_count * cut, 0, cut, home, rest)]
    high += [mix(time_count * cut, z, 3 * cut - rest, far, rest) for z in hops]

    def with_other(values):
        return [side for v in values for side in (v, travel(v, ("pol",), (1,)))]

    early = with_other([jnp.stack([early[p] for p in pairs])])
    blocks, held = after(high[1:], [low[2], low[1], early[1]])
    low[2], low[1], early[1] = held
    moved = {z: over(blocks[z - 1], 0, z) for z in (2, 1, 3)}
    high = [high[0]] + [moved[z] for z in (1, 2, 3)]
    low = jnp.stack(low).reshape(2 * time_count, cut, 2, ROWS, LANES)
    visibility = correlate_tiles(
        place, tables_of_tiles, early + with_other([low]),
        [0, 0], width, 0, cut, bands, None,
    )
    high, (visibility,) = after(high, [visibility])
    high = jnp.stack(high).reshape(2 * time_count, rest, 2, ROWS, LANES)
    return correlate_tiles(
        place, tables_of_tiles, early + with_other([high]),
        [cut, 0], width, cut, rest, bands, visibility,
    )


def on_device(voltages, taps_filter, tile_a, tile_b, tile_owner, tile_flags):
    taps, length = taps_filter.shape
    frames = voltages.shape[3] // length
    time_count = lax.axis_size("tm")
    fits = (
        length == RADIX * LANES
        and AVG * time_count * frames == LANES
        and 2 * tile_a.shape[1] == LANES
        and voltages.shape[2] == 2 * time_count * ROWS
        and (lax.axis_size("chan"), time_count) == (2, 4)
    )
    form = on_device_chunks if fits else on_device_any
    return form(voltages, taps_filter, tile_a, tile_b, tile_owner, tile_flags)


def solution(mesh):
    return jax.shard_map(
        on_device,
        mesh=mesh,
        in_specs=(P("grp", "pol", "chan", "tm"), P(), P(), P(), P(), P()),
        out_specs=P("pol", ("chan", "tm"), "grp", None, None, None),
        check_vma=False,
    )
```

profile of v0, /device:TPU:11, one launch (start us, length us, event | category | flops | bytes accessed | tf_op | source)
XLA Modules:
  0.0 221.1 jit_solution(2973081733660666676)
XLA Ops:
  2.5 3.0 %constant_dynamic-slice_fusion = (bf16[2,16,8192]{2,1,0:T(8,128)(2,1)}, bf16[2,16,8192]{2,1,0:T(8,128)(2,1)S(1)}, bf16[2,16,8192]{2,1,0:T(8,128)(2,1)S(1)}, bf16[2,16,8192]{2,1,0:T(8,128)(2,1)}, bf16[2,16,8192]{2,1,0:T(8,128)(2,1)}) fusion(bf16[2,128,8192]{2,1,0:T(8,128)(2,1)} %bitcast.90, s32[]{:T(128)S(6)} %select_n.109, s32[]{:T(128)S(6)} %select_n.108, ...), kind=kLoop, calls=%fused_computation.137 | loop fusion | bytes 5242900 | tf_op jit(solution)/shard_map/dynamic_slice | solution.py:490
  7.3 6.6 %collective-permute-done.refs_2_ = bf16[2,16,8192]{2,1,0:T(8,128)(2,1)S(1)} collective-permute-done((bf16[2,16,8192]{2,1,0:T(8,128)(2,1)S(1)}, bf16[2,16,8192]{2,1,0:T(8,128)(2,1)S(1)}, u32[]{:S(2)}, u32[]{:S(2)}) %collective-permute-start) | collective-permute-done | bytes 524320 | tf_op jit(solution)/shard_map/ppermute | solution.py:483
  13.9 2.1 collective-permute-start.2
  16.1 30.7 %collective-permute-done.1.refs_3_ = bf16[2,16,8192]{2,1,0:T(8,128)(2,1)S(1)} collective-permute-done((bf16[2,16,8192]{2,1,0:T(8,128)(2,1)S(1)}, bf16[2,16,8192]{2,1,0:T(8,128)(2,1)S(1)}, u32[]{:S(2)}, u32[]{:S(2)}) %collective-permute-start.1) | collective-permute-done | bytes 524320 | tf_op jit(solution)/shard_map/ppermute | solution.py:483
  48.8 9.7 %collective-permute-done.3.refs_2_ = bf16[2,16,8192]{2,1,0:T(8,128)(2,1)S(1)} collective-permute-done((bf16[2,16,8192]{2,1,0:T(8,128)(2,1)}, bf16[2,16,8192]{2,1,0:T(8,128)(2,1)S(1)}, u32[]{:S(2)}, u32[]{:S(2)}) %collective-permute-start.3) | collective-permute-done | bytes 524320 | tf_op jit(solution)/shard_map/ppermute | solution.py:483
  58.4 4.1 %collective-permute-start.4 = (bf16[2,16,8192]{2,1,0:T(8,128)(2,1)}, bf16[2,16,8192]{2,1,0:T(8,128)(2,1)S(1)}, u32[]{:S(2)}, u32[]{:S(2)}) collective-permute-start(bf16[2,16,8192]{2,1,0:T(8,128)(2,1)} %get-tuple-element.72), channel_id=1, source_target_pairs={{0,4},{2,6},{4,0},{6,2},{8,12},{10,14},{12,8},{14,10},{1,5},{3,7},... | collective-permute-start | bytes 1572872 | tf_op jit(solution)/shard_map/ppermute | solution.py:483
  62.6 2.2 copy-done
  64.8 15.6 %channelise.2 = (bf16[1024,128]{1,0:T(8,128)(2,1)S(1)}, bf16[1024,128]{1,0:T(8,128)(2,1)S(1)}, bf16[1024,128]{1,0:T(8,128)(2,1)S(1)}, bf16[1024,128]{1,0:T(8,128...) custom-call(s32[3]{0:T(128)S(1)} %pad_add_fusion.refs_0_, ...), custom_call_target="tpu_custom_call" | custom-call | flops 8999999488 | bytes 4194304 | tf_op jit(solution)/shard_map/channelise/pallas_call | solution.py:276
  80.3 13.3 %collective-permute-done.4.refs_3_ = bf16[2,16,8192]{2,1,0:T(8,128)(2,1)S(1)} collective-permute-done((bf16[2,16,8192]{2,1,0:T(8,128)(2,1)}, bf16[2,16,8192]{2,1,0:T(8,128)(2,1)S(1)}, u32[]{:S(2)}, u32[]{:S(2)}) %collective-permute-start.4) | collective-permute-done | bytes 524320 | tf_op jit(solution)/shard_map/ppermute | solution.py:483
  93.6 1.9 collective-permute-start.7
  97.3 4.2 %collective-permute-start.10 = (bf16[32,2,16,128]{3,2,1,0:T(8,128)(2,1)S(1)}, bf16[32,2,16,128]{3,2,1,0:T(8,128)(2,1)S(1)}, u32[]{:S(2)}, u32[]{:S(2)}) collective-permute-start(bf16[32,2,16,128]{3,2,1,0:T(8,128)(2,1)S(1)} %bitcast.101), channel_id=1, source_target_pairs={{0,14},{2,8},{4,10},{6,12},{8,6},{10,0},{12,2},{14,4},{1,15},{3,9}... | collective-permute-start | bytes 786440 | tf_op jit(solution)/shard_map/ppermute | solution.py:483
  101.5 15.6 %channelise.3 = (bf16[4096,128]{1,0:T(8,128)(2,1)S(1)}, bf16[3072,128]{1,0:T(8,128)(2,1)S(1)}, bf16[1024,128]{1,0:T(8,128)(2,1)S(1)}) custom-call(s32[3]{0:T(128)S(1)} %pad_add_fusion.refs_0_, bf16[2,128,8192]{2,1,0:T(8,128)(2,1)S(1)} %bitcast.92, bf16[2,16,8192]{2,1,0:T(8,128)(2,1)S(1)} %collective-permute-done.3.refs_2_, ...), custom_call_target="tpu_custom_call" | custom-call | flops 8999999488 | bytes 4194304 | tf_op jit(solution)/shard_map/channelise/pallas_call | solution.py:276
  117.8 3.0 %collective-permute-start.13 = (bf16[32,2,16,128]{3,2,1,0:T(8,128)(2,1)S(1)}, bf16[32,2,16,128]{3,2,1,0:T(8,128)(2,1)S(1)}, u32[]{:S(2)}, u32[]{:S(2)}) collective-permute-start(bf16[32,2,16,128]{3,2,1,0:T(8,128)(2,1)S(1)} %bitcast.98), channel_id=1, source_target_pairs={{0,12},{2,14},{4,8},{6,10},{8,4},{10,6},{12,0},{14,2},{1,13},{3,15... | collective-permute-start | bytes 786440 | tf_op jit(solution)/shard_map/ppermute | solution.py:483
  120.8 3.1 %collective-permute-done.10 = bf16[32,2,16,128]{3,2,1,0:T(8,128)(2,1)S(1)} collective-permute-done((bf16[32,2,16,128]{3,2,1,0:T(8,128)(2,1)S(1)}, bf16[32,2,16,128]{3,2,1,0:T(8,128)(2,1)S(1)}, u32[]{:S(2)}, u32[]{:S(2)}) %collective-permute-start.10) | collective-permute-done | bytes 262176 | tf_op jit(solution)/shard_map/ppermute | solution.py:483
  125.1 4.2 %collective-permute-done.6 = bf16[32,2,16,128]{3,2,1,0:T(8,128)(2,1)S(1)} collective-permute-done((bf16[32,2,16,128]{3,2,1,0:T(8,128)(2,1)S(1)}, bf16[32,2,16,128]{3,2,1,0:T(8,128)(2,1)S(1)}, u32[]{:S(2)}, u32[]{:S(2)}) %collective-permute-start.6) | collective-permute-done | bytes 262176 | tf_op jit(solution)/shard_map/ppermute | solution.py:483
  129.4 21.7 %collective-permute-done.11 = bf16[96,2,16,128]{3,2,1,0:T(8,128)(2,1)S(1)} collective-permute-done((bf16[96,2,16,128]{3,2,1,0:T(8,128)(2,1)S(1)}, bf16[96,2,16,128]{3,2,1,0:T(8,128)(2,1)S(1)}, u32[]{:S(2)}, u32[]{:S(2)}) %collective-permute-start.11) | collective-permute-done | bytes 786464 | tf_op jit(solution)/shard_map/ppermute | solution.py:483
  153.6 14.8 %collective-permute-done.17 = bf16[2,20,2,16,128]{4,3,2,1,0:T(8,128)(2,1)S(1)} collective-permute-done((bf16[2,20,2,16,128]{4,3,2,1,0:T(8,128)(2,1)S(1)}, bf16[2,20,2,16,128]{4,3,2,1,0:T(8,128)(2,1)S(1)}, u32[]{:S(2)}, u32[]{:S(2)}) %collective-permute-start.17) | collective-permute-done | bytes 327712 | tf_op jit(solution)/shard_map/ppermute | solution.py:483
  171.8 3.7 %collective-permute-done.18 = bf16[32,2,16,128]{3,2,1,0:T(8,128)(2,1)S(1)} collective-permute-done((bf16[32,2,16,128]{3,2,1,0:T(8,128)(2,1)S(1)}, bf16[32,2,16,128]{3,2,1,0:T(8,128)(2,1)S(1)}, u32[]{:S(2)}, u32[]{:S(2)}) %collective-permute-start.18) | collective-permute-done | bytes 262176 | tf_op jit(solution)/shard_map/ppermute | solution.py:483
  175.5 9.9 %collective-permute-done.15 = bf16[2,20,2,16,128]{4,3,2,1,0:T(8,128)(2,1)S(1)} collective-permute-done((bf16[2,20,2,16,128]{4,3,2,1,0:T(8,128)(2,1)S(1)}, bf16[2,20,2,16,128]{4,3,2,1,0:T(8,128)(2,1)S(1)}, u32[]{:S(2)}, u32[]{:S(2)}) %collective-permute-start.15) | collective-permute-done | bytes 327712 | tf_op jit(solution)/shard_map/ppermute | solution.py:483
  187.7 4.0 %collective-permute-start.20 = (bf16[2,12,2,16,128]{4,3,2,1,0:T(8,128)(2,1)S(1)}, bf16[2,12,2,16,128]{4,3,2,1,0:T(8,128)(2,1)S(1)}, u32[]{:S(2)}, u32[]{:S(2)}) collective-permute-start(bf16[2,12,2,16,128]{4,3,2,1,0:T(8,128)(2,1)S(1)} %pad_maximum_fusion.6), channel_id=1, source_target_pairs={{0,4},{2,6},{4,0},{6,2},{8,12},{10,14},{12,8},{14,10},{1,5},{3,7},... | collective-permute-start | bytes 589832 | tf_op jit(solution)/shard_map/ppermute | solution.py:483
  191.7 14.5 %correlate.2.refs_8_ = f32[8,32,2,2,64,128]{5,4,3,2,1,0:T(8,128)} custom-call(s32[3]{0:T(128)S(1)} %pad_add_fusion.refs_0_, bf16[512,256]{1,0:T(8,128)(2,1)S(1)} %fusion.1.refs_1_, bf16[2,256,512]{2,1,0:T(8,128)(2,1)S(1)} %fusion.refs_2_, f32[8,256]{1,0:T(8,128)S(1)} %tile.10.refs_3_, ...), custom_call_target="tpu_custom_call" | custom-call | flops 8125000192 | bytes 27525120 | tf_op jit(solution)/shard_map/correlate/pallas_call | solution.py:401
  206.3 2.3 %collective-permute-done.21 = bf16[2,12,2,16,128]{4,3,2,1,0:T(8,128)(2,1)S(1)} collective-permute-done((bf16[2,12,2,16,128]{4,3,2,1,0:T(8,128)(2,1)S(1)}, bf16[2,12,2,16,128]{4,3,2,1,0:T(8,128)(2,1)S(1)}, u32[]{:S(2)}, u32[]{:S(2)}) %collective-permute-start.21) | collective-permute-done | bytes 196640 | tf_op jit(solution)/shard_map/ppermute | solution.py:483
  209.6 1.9 collective-permute-done.23.refs_7_
  211.5 9.6 %correlate.3 = f32[8,32,2,2,64,128]{5,4,3,2,1,0:T(8,128)} custom-call(s32[3]{0:T(128)S(1)} %pad_add_fusion.refs_0_, bf16[512,256]{1,0:T(8,128)(2,1)S(1)} %fusion.1.refs_1_, bf16[2,256,512]{2,1,0:T(8,128)(2,1)S(1)} %fusion.refs_2_, f32[8,256]{1,0:T(8,128)S(1)} %tile.10.refs_3_, ...), custom_call_target="tpu_custom_call", output_to_operand_aliasing={{}: (8, {})} | custom-call | flops 4874999808 | bytes 16515072 | tf_op jit(solution)/shard_map/correlate/pallas_call | solution.py:401
  (91 shorter events, 19.2 us)
Async XLA Ops:
  1.1 12.8 %collective-permute-start = (bf16[2,16,8192]{2,1,0:T(8,128)(2,1)S(1)}, bf16[2,16,8192]{2,1,0:T(8,128)(2,1)S(1)}, u32[]{:S(2)}, u32[]{:S(2)}) collective-permute-start(bf16[2,16,8192]{2,1,0:T(8,128)(2,1)S(1)} %dynamic-slice_bitcast_fusion), channel_id=1, source_target_pairs={{0,2},{2,4},{4,6},{6,0},{8,10},{10,12},{12,14},{14,8},{1,3},{3,5},... | collective-permute-start | bytes 1572872 | tf_op jit(solution)/shard_map/ppermute | solution.py:483
  5.5 41.3 %collective-permute-start.1 = (bf16[2,16,8192]{2,1,0:T(8,128)(2,1)S(1)}, bf16[2,16,8192]{2,1,0:T(8,128)(2,1)S(1)}, u32[]{:S(2)}, u32[]{:S(2)}) collective-permute-start(bf16[2,16,8192]{2,1,0:T(8,128)(2,1)S(1)} %get-tuple-element.119), channel_id=1, source_target_pairs={{0,4},{2,6},{4,0},{6,2},{8,12},{10,14},{12,8},{14,10},{1,5},{3,7},... | collective-permute-start | bytes 1572872 | tf_op jit(solution)/shard_map/ppermute | solution.py:483
  13.9 33.3 %collective-permute-start.2 = (bf16[2,16,8192]{2,1,0:T(8,128)(2,1)}, bf16[2,16,8192]{2,1,0:T(8,128)(2,1)S(1)}, u32[]{:S(2)}, u32[]{:S(2)}) collective-permute-start(bf16[2,16,8192]{2,1,0:T(8,128)(2,1)} %get-tuple-element.65), channel_id=1, source_target_pairs={{0,6},{2,0},{4,2},{6,4},{8,14},{10,8},{12,10},{14,12},{1,7},{3,1},... | collective-permute-start | bytes 1572872 | tf_op jit(solution)/shard_map/ppermute | solution.py:483
  46.7 11.7 %collective-permute-start.3 = (bf16[2,16,8192]{2,1,0:T(8,128)(2,1)}, bf16[2,16,8192]{2,1,0:T(8,128)(2,1)S(1)}, u32[]{:S(2)}, u32[]{:S(2)}) collective-permute-start(bf16[2,16,8192]{2,1,0:T(8,128)(2,1)} %get-tuple-element.71), channel_id=1, source_target_pairs={{0,2},{2,4},{4,6},{6,0},{8,10},{10,12},{12,14},{14,8},{1,3},{3,5},... | collective-permute-start | bytes 1572872 | tf_op jit(solution)/shard_map/ppermute | solution.py:483
  47.3 54.2 %collective-permute-start.5 = (bf16[2,16,8192]{2,1,0:T(8,128)(2,1)S(1)}, bf16[2,16,8192]{2,1,0:T(8,128)(2,1)S(1)}, u32[]{:S(2)}, u32[]{:S(2)}) collective-permute-start(bf16[2,16,8192]{2,1,0:T(8,128)(2,1)S(1)} %get-tuple-element.82), channel_id=1, source_target_pairs={{0,6},{2,0},{4,2},{6,4},{8,14},{10,8},{12,10},{14,12},{1,7},{3,1},... | collective-permute-start | bytes 1572872 | tf_op jit(solution)/shard_map/ppermute | solution.py:483
  58.4 35.2 %collective-permute-start.4 = (bf16[2,16,8192]{2,1,0:T(8,128)(2,1)}, bf16[2,16,8192]{2,1,0:T(8,128)(2,1)S(1)}, u32[]{:S(2)}, u32[]{:S(2)}) collective-permute-start(bf16[2,16,8192]{2,1,0:T(8,128)(2,1)} %get-tuple-element.72), channel_id=1, source_target_pairs={{0,4},{2,6},{4,0},{6,2},{8,12},{10,14},{12,8},{14,10},{1,5},{3,7},... | collective-permute-start | bytes 1572872 | tf_op jit(solution)/shard_map/ppermute | solution.py:483
  93.6 23.8 %collective-permute-start.7 = (bf16[32,2,16,128]{3,2,1,0:T(8,128)(2,1)S(1)}, bf16[32,2,16,128]{3,2,1,0:T(8,128)(2,1)S(1)}, u32[]{:S(2)}, u32[]{:S(2)}) collective-permute-start(bf16[32,2,16,128]{3,2,1,0:T(8,128)(2,1)S(1)} %bitcast.104), channel_id=1, source_target_pairs={{0,2},{2,4},{4,6},{6,0},{8,10},{10,12},{12,14},{14,8},{1,3},{3,5},... | collective-permute-start | bytes 786440 | tf_op jit(solution)/shard_map/ppermute | solution.py:483
  95.5 22.3 %collective-permute-start.8 = (bf16[32,2,16,128]{3,2,1,0:T(8,128)(2,1)S(1)}, bf16[32,2,16,128]{3,2,1,0:T(8,128)(2,1)S(1)}, u32[]{:S(2)}, u32[]{:S(2)}) collective-permute-start(bf16[32,2,16,128]{3,2,1,0:T(8,128)(2,1)S(1)} %bitcast.103), channel_id=1, source_target_pairs={{0,10},{2,12},{4,14},{6,8},{8,2},{10,4},{12,6},{14,0},{1,11},{3,13... | collective-permute-start | bytes 786440 | tf_op jit(solution)/shard_map/ppermute | solution.py:483
  96.9 23.9 %collective-permute-start.9 = (bf16[32,2,16,128]{3,2,1,0:T(8,128)(2,1)S(1)}, bf16[32,2,16,128]{3,2,1,0:T(8,128)(2,1)S(1)}, u32[]{:S(2)}, u32[]{:S(2)}) collective-permute-start(bf16[32,2,16,128]{3,2,1,0:T(8,128)(2,1)S(1)} %bitcast.102), channel_id=1, source_target_pairs={{0,6},{2,0},{4,2},{6,4},{8,14},{10,8},{12,10},{14,12},{1,7},{3,1},... | collective-permute-start | bytes 786440 | tf_op jit(solution)/shard_map/ppermute | solution.py:483
  97.3 26.5 %collective-permute-start.10 = (bf16[32,2,16,128]{3,2,1,0:T(8,128)(2,1)S(1)}, bf16[32,2,16,128]{3,2,1,0:T(8,128)(2,1)S(1)}, u32[]{:S(2)}, u32[]{:S(2)}) collective-permute-start(bf16[32,2,16,128]{3,2,1,0:T(8,128)(2,1)S(1)} %bitcast.101), channel_id=1, source_target_pairs={{0,14},{2,8},{4,10},{6,12},{8,6},{10,0},{12,2},{14,4},{1,15},{3,9}... | collective-permute-start | bytes 786440 | tf_op jit(solution)/shard_map/ppermute | solution.py:483
  117.0 12.2 %collective-permute-start.6 = (bf16[32,2,16,128]{3,2,1,0:T(8,128)(2,1)S(1)}, bf16[32,2,16,128]{3,2,1,0:T(8,128)(2,1)S(1)}, u32[]{:S(2)}, u32[]{:S(2)}) collective-permute-start(bf16[32,2,16,128]{3,2,1,0:T(8,128)(2,1)S(1)} %bitcast.100), channel_id=1, source_target_pairs={{0,8},{2,10},{4,12},{6,14},{8,0},{10,2},{12,4},{14,6},{1,9},{3,11}... | collective-permute-start | bytes 786440 | tf_op jit(solution)/shard_map/ppermute | solution.py:483
  117.4 33.8 %collective-permute-start.12 = (bf16[32,2,16,128]{3,2,1,0:T(8,128)(2,1)S(1)}, bf16[32,2,16,128]{3,2,1,0:T(8,128)(2,1)S(1)}, u32[]{:S(2)}, u32[]{:S(2)}) collective-permute-start(bf16[32,2,16,128]{3,2,1,0:T(8,128)(2,1)S(1)} %bitcast.99), channel_id=1, source_target_pairs={{0,4},{2,6},{4,0},{6,2},{8,12},{10,14},{12,8},{14,10},{1,5},{3,7},... | collective-permute-start | bytes 786440 | tf_op jit(solution)/shard_map/ppermute | solution.py:483
  117.8 33.5 %collective-permute-start.13 = (bf16[32,2,16,128]{3,2,1,0:T(8,128)(2,1)S(1)}, bf16[32,2,16,128]{3,2,1,0:T(8,128)(2,1)S(1)}, u32[]{:S(2)}, u32[]{:S(2)}) collective-permute-start(bf16[32,2,16,128]{3,2,1,0:T(8,128)(2,1)S(1)} %bitcast.98), channel_id=1, source_target_pairs={{0,12},{2,14},{4,8},{6,10},{8,4},{10,6},{12,0},{14,2},{1,13},{3,15... | collective-permute-start | bytes 786440 | tf_op jit(solution)/shard_map/ppermute | solution.py:483
  123.9 27.3 %collective-permute-start.11 = (bf16[96,2,16,128]{3,2,1,0:T(8,128)(2,1)S(1)}, bf16[96,2,16,128]{3,2,1,0:T(8,128)(2,1)S(1)}, u32[]{:S(2)}, u32[]{:S(2)}) collective-permute-start(bf16[96,2,16,128]{3,2,1,0:T(8,128)(2,1)S(1)} %bitcast.96), channel_id=1, source_target_pairs={{0,8},{2,10},{4,12},{6,14},{8,0},{10,2},{12,4},{14,6},{1,9},{3,11}... | collective-permute-start | bytes 2359304 | tf_op jit(solution)/shard_map/ppermute | solution.py:483
  151.4 34.0 %collective-permute-start.16 = (bf16[8,32,2,16,128]{4,3,2,1,0:T(8,128)(2,1)S(1)}, bf16[8,32,2,16,128]{4,3,2,1,0:T(8,128)(2,1)S(1)}, u32[]{:S(2)}, u32[]{:S(2)}) collective-permute-start(bf16[8,32,2,16,128]{4,3,2,1,0:T(8,128)(2,1)S(1)} %bitcast_dynamic-update-slice_fusion.refs_4_), channel_id=1, source_target_pairs={{0,1},{1,0},{2,3},{3,2},{4,5},{5,4},{6,7},{7,6},{8,9},{9,8},{10,11... | collective-permute-start | bytes 6291464 | tf_op jit(solution)/shard_map/ppermute | solution.py:483
  152.0 18.0 %collective-permute-start.14 = (bf16[2,20,2,16,128]{4,3,2,1,0:T(8,128)(2,1)S(1)}, bf16[2,20,2,16,128]{4,3,2,1,0:T(8,128)(2,1)S(1)}, u32[]{:S(2)}, u32[]{:S(2)}) collective-permute-start(bf16[2,20,2,16,128]{4,3,2,1,0:T(8,128)(2,1)S(1)} %pad_maximum_fusion.2), channel_id=1, source_target_pairs={{0,2},{2,4},{4,6},{6,0},{8,10},{10,12},{12,14},{14,8},{1,3},{3,5},... | collective-permute-start | bytes 983048 | tf_op jit(solution)/shard_map/ppermute | solution.py:483
  152.1 16.3 %collective-permute-start.17 = (bf16[2,20,2,16,128]{4,3,2,1,0:T(8,128)(2,1)S(1)}, bf16[2,20,2,16,128]{4,3,2,1,0:T(8,128)(2,1)S(1)}, u32[]{:S(2)}, u32[]{:S(2)}) collective-permute-start(bf16[2,20,2,16,128]{4,3,2,1,0:T(8,128)(2,1)S(1)} %pad_maximum_fusion.3), channel_id=1, source_target_pairs={{0,6},{2,0},{4,2},{6,4},{8,14},{10,8},{12,10},{14,12},{1,7},{3,1},... | collective-permute-start | bytes 983048 | tf_op jit(solution)/shard_map/ppermute | solution.py:483
  168.4 7.1 %collective-permute-start.18 = (bf16[32,2,16,128]{3,2,1,0:T(8,128)(2,1)S(1)}, bf16[32,2,16,128]{3,2,1,0:T(8,128)(2,1)S(1)}, u32[]{:S(2)}, u32[]{:S(2)}) collective-permute-start(bf16[32,2,16,128]{3,2,1,0:T(8,128)(2,1)S(1)} %bitcast.97), channel_id=1, source_target_pairs={{0,8},{2,10},{4,12},{6,14},{8,0},{10,2},{12,4},{14,6},{1,9},{3,11}... | collective-permute-start | bytes 786440 | tf_op jit(solution)/shard_map/ppermute | solution.py:483
  170.0 15.4 %collective-permute-start.15 = (bf16[2,20,2,16,128]{4,3,2,1,0:T(8,128)(2,1)S(1)}, bf16[2,20,2,16,128]{4,3,2,1,0:T(8,128)(2,1)S(1)}, u32[]{:S(2)}, u32[]{:S(2)}) collective-permute-start(bf16[2,20,2,16,128]{4,3,2,1,0:T(8,128)(2,1)S(1)} %pad_maximum_fusion.4), channel_id=1, source_target_pairs={{0,4},{2,6},{4,0},{6,2},{8,12},{10,14},{12,8},{14,10},{1,5},{3,7},... | collective-permute-start | bytes 983048 | tf_op jit(solution)/shard_map/ppermute | solution.py:483
  185.6 6.1 %collective-permute-start.22 = (bf16[8,20,2,16,128]{4,3,2,1,0:T(8,128)(2,1)S(1)}, bf16[8,20,2,16,128]{4,3,2,1,0:T(8,128)(2,1)S(1)}, u32[]{:S(2)}, u32[]{:S(2)}) collective-permute-start(bf16[8,20,2,16,128]{4,3,2,1,0:T(8,128)(2,1)S(1)} %bitcast.86), channel_id=1, source_target_pairs={{0,1},{1,0},{2,3},{3,2},{4,5},{5,4},{6,7},{7,6},{8,9},{9,8},{10,11... | collective-permute-start | bytes 3932168 | tf_op jit(solution)/shard_map/ppermute | solution.py:483
  186.2 20.0 %collective-permute-start.19 = (bf16[2,12,2,16,128]{4,3,2,1,0:T(8,128)(2,1)S(1)}, bf16[2,12,2,16,128]{4,3,2,1,0:T(8,128)(2,1)S(1)}, u32[]{:S(2)}, u32[]{:S(2)}) collective-permute-start(bf16[2,12,2,16,128]{4,3,2,1,0:T(8,128)(2,1)S(1)} %pad_maximum_fusion.5), channel_id=1, source_target_pairs={{0,2},{2,4},{4,6},{6,0},{8,10},{10,12},{12,14},{14,8},{1,3},{3,5},... | collective-permute-start | bytes 589832 | tf_op jit(solution)/shard_map/ppermute | solution.py:483
  187.7 18.6 %collective-permute-start.20 = (bf16[2,12,2,16,128]{4,3,2,1,0:T(8,128)(2,1)S(1)}, bf16[2,12,2,16,128]{4,3,2,1,0:T(8,128)(2,1)S(1)}, u32[]{:S(2)}, u32[]{:S(2)}) collective-permute-start(bf16[2,12,2,16,128]{4,3,2,1,0:T(8,128)(2,1)S(1)} %pad_maximum_fusion.6), channel_id=1, source_target_pairs={{0,4},{2,6},{4,0},{6,2},{8,12},{10,14},{12,8},{14,10},{1,5},{3,7},... | collective-permute-start | bytes 589832 | tf_op jit(solution)/shard_map/ppermute | solution.py:483
  191.7 16.9 %collective-permute-start.21 = (bf16[2,12,2,16,128]{4,3,2,1,0:T(8,128)(2,1)S(1)}, bf16[2,12,2,16,128]{4,3,2,1,0:T(8,128)(2,1)S(1)}, u32[]{:S(2)}, u32[]{:S(2)}) collective-permute-start(bf16[2,12,2,16,128]{4,3,2,1,0:T(8,128)(2,1)S(1)} %pad_maximum_fusion.7), channel_id=1, source_target_pairs={{0,6},{2,0},{4,2},{6,4},{8,14},{10,8},{12,10},{14,12},{1,7},{3,1},... | collective-permute-start | bytes 589832 | tf_op jit(solution)/shard_map/ppermute | solution.py:483
  208.7 2.8 %collective-permute-start.23 = (bf16[8,12,2,16,128]{4,3,2,1,0:T(8,128)(2,1)S(1)}, bf16[8,12,2,16,128]{4,3,2,1,0:T(8,128)(2,1)S(1)}, u32[]{:S(2)}, u32[]{:S(2)}) collective-permute-start(bf16[8,12,2,16,128]{4,3,2,1,0:T(8,128)(2,1)S(1)} %bitcast.88), channel_id=1, source_target_pairs={{0,1},{1,0},{2,3},{3,2},{4,5},{5,4},{6,7},{7,6},{8,9},{9,8},{10,11... | collective-permute-start | bytes 2359304 | tf_op jit(solution)/shard_map/ppermute | solution.py:483
  (8 other events, 200.0 us)
where the time goes:
time: 221 us
  waiting for transfers between devices  122 us (55%)
  Pallas kernels  55.3 us (25%)
  starting transfers between devices  35.2 us (16%)
  local copies, waits for them, and re-layouts  7.09 us (3%)
    ppermute x24, waiting for transfers between devices, travel(): return lax.ppermute(value, axes, pairs)  122 us
    ppermute x24, starting transfers between devices, travel(): return lax.ppermute(value, axes, pairs)  35.2 us
    pallas_call x2, Pallas kernels, channelise(): pl.pallas_call(lambda *refs: channelise_kernel(frames, chunk, columns, pl...  31.1 us
    pallas_call x2, Pallas kernels, correlate_tiles(): pl.pallas_call(lambda *refs: correlate_kernel(starts, width, *refs), grid...  24.2 us
  transfers between devices with their start and end apart: 24, of which 12 were waited for; matrix products, arithmetic and copies ran while one was open for 2% of the time, Pallas kernels for 21%

commit v1 on v0

--- a/solution.py
+++ b/solution.py
@@ -254,7 +254,7 @@
 
     share = w_ref.shape[0] // (columns * sources)
     band_rows = 2 * ROWS
-    piece = 4 * band_rows
+    piece = 2 * band_rows
     for blocks, out_ref in zip(plan, out_refs):
         at = 0
         for across, along, start, stop in blocks:
@@ -500,7 +500,7 @@
     def columns(near, far):
         return jnp.stack([near, far])
 
-    cut = bands * 5 // 8
+    cut = bands * 9 // 16
     rest = bands - cut
     pairs = [(x, z) for z in range(time_count) for x in range(chan_count)]
     early_pairs = [(x, z) for z in (1, 3) for x in range(2)]
@@ -539,12 +539,11 @@
         return columns(near[first : first + count], other[second : second + count])
 
     blocks = {z: mix(0, z, -cut, far, cut) for z in hops}
-    (blocks[1], blocks[3]), held = after([blocks[1], blocks[3]], [early[p] for p in late_pairs[:1]])
+    order = [2, 1, 3]
+    values, held = after([blocks[z] for z in order], [early[p] for p in late_pairs[:1]])
     early.update(zip(late_pairs[:1], held))
-    one, three = over(blocks[1], 0, 1), over(blocks[3], 0, 3)
-    (block,), (one,) = after([blocks[2]], [one])
-    two = over(block, 0, 2)
-    (home,), (three,) = after([home], [three])
+    two, one, three = (over(value, 0, z) for value, z in zip(values, order))
+    (home,), (one,) = after([home], [one])
     home = over(home, 1, 0)
     low = [mix(0, 0, 0, home, cut), one, two, three]
     high = [mix(time_count * cut, 0, cut, home, rest)]

time: 221 us -> 217 us (0.982)
  starting transfers between devices: 35.2 us -> 29.6 us
    ppermute x24, starting transfers between devices: 35.2 us -> 29.6 us  [travel(): return lax.ppermute(value, axes, pairs)]
  transfers between devices with their start and end apart: 24 -> 24, of which waited for: 12 -> 15; matrix products, arithmetic and copies ran while one was open for 2% -> 2% of each run, Pallas kernels for 21% -> 21%
where the time goes in v1:
time: 217 us; the launch traced here: 216 us
  waiting for transfers between devices  122 us (56%)
  Pallas kernels  55.4 us (26%)
  starting transfers between devices  29.6 us (14%)
  local copies, waits for them, and re-layouts  7.09 us (3%)
    ppermute x24, waiting for transfers between devices, travel(): return lax.ppermute(value, axes, pairs)  122 us
    pallas_call x2, Pallas kernels, channelise(): pl.pallas_call(lambda *refs: channelise_kernel(frames, chunk, columns, pl...  31.1 us
    ppermute x24, starting transfers between devices, travel(): return lax.ppermute(value, axes, pairs)  29.6 us
    pallas_call x2, Pallas kernels, correlate_tiles(): pl.pallas_call(lambda *refs: correlate_kernel(starts, width, *refs), grid...  24.3 us
  transfers between devices with their start and end apart: 24, of which 15 were waited for; matrix products, arithmetic and copies ran while one was open for 2% of the time, Pallas kernels for 21%

profile of v1, /device:TPU:11, one launch (start us, length us, event | category | flops | bytes accessed | tf_op | source)
XLA Modules:
  0.0 216.2 jit_solution(14326267122299054144)
XLA Ops:
  2.5 3.0 %constant_dynamic-slice_fusion = (bf16[2,16,8192]{2,1,0:T(8,128)(2,1)}, bf16[2,16,8192]{2,1,0:T(8,128)(2,1)S(1)}, bf16[2,16,8192]{2,1,0:T(8,128)(2,1)S(1)}, bf16[2,16,8192]{2,1,0:T(8,128)(2,1)}, bf16[2,16,8192]{2,1,0:T(8,128)(2,1)}) fusion(bf16[2,128,8192]{2,1,0:T(8,128)(2,1)} %bitcast.90, s32[]{:T(128)S(6)} %select_n.109, s32[]{:T(128)S(6)} %select_n.108, ...), kind=kLoop, calls=%fused_computation.137 | loop fusion | bytes 5242900 | tf_op jit(solution)/shard_map/dynamic_slice | solution.py:490
  7.3 6.6 %collective-permute-done.refs_2_ = bf16[2,16,8192]{2,1,0:T(8,128)(2,1)S(1)} collective-permute-done((bf16[2,16,8192]{2,1,0:T(8,128)(2,1)S(1)}, bf16[2,16,8192]{2,1,0:T(8,128)(2,1)S(1)}, u32[]{:S(2)}, u32[]{:S(2)}) %collective-permute-start) | collective-permute-done | bytes 524320 | tf_op jit(solution)/shard_map/ppermute | solution.py:483
  13.9 2.1 collective-permute-start.2
  16.1 30.7 %collective-permute-done.1.refs_3_ = bf16[2,16,8192]{2,1,0:T(8,128)(2,1)S(1)} collective-permute-done((bf16[2,16,8192]{2,1,0:T(8,128)(2,1)S(1)}, bf16[2,16,8192]{2,1,0:T(8,128)(2,1)S(1)}, u32[]{:S(2)}, u32[]{:S(2)}) %collective-permute-start.1) | collective-permute-done | bytes 524320 | tf_op jit(solution)/shard_map/ppermute | solution.py:483
  48.8 9.7 %collective-permute-done.3.refs_2_ = bf16[2,16,8192]{2,1,0:T(8,128)(2,1)S(1)} collective-permute-done((bf16[2,16,8192]{2,1,0:T(8,128)(2,1)}, bf16[2,16,8192]{2,1,0:T(8,128)(2,1)S(1)}, u32[]{:S(2)}, u32[]{:S(2)}) %collective-permute-start.3) | collective-permute-done | bytes 524320 | tf_op jit(solution)/shard_map/ppermute | solution.py:483
  58.4 4.1 %collective-permute-start.4 = (bf16[2,16,8192]{2,1,0:T(8,128)(2,1)}, bf16[2,16,8192]{2,1,0:T(8,128)(2,1)S(1)}, u32[]{:S(2)}, u32[]{:S(2)}) collective-permute-start(bf16[2,16,8192]{2,1,0:T(8,128)(2,1)} %get-tuple-element.71), channel_id=1, source_target_pairs={{0,4},{2,6},{4,0},{6,2},{8,12},{10,14},{12,8},{14,10},{1,5},{3,7},... | collective-permute-start | bytes 1572872 | tf_op jit(solution)/shard_map/ppermute | solution.py:483
  62.6 2.2 %copy-done = bf16[2,1,128,8192]{3,2,1,0:T(8,128)(2,1)S(1)} copy-done((bf16[2,1,128,8192]{3,2,1,0:T(8,128)(2,1)S(1)}, bf16[2,1,128,8192]{3,2,1,0:T(8,128)(2,1)}, u32[]{:S(2)}) %copy-start) | copy-done | bytes 4194328
  64.8 15.6 %channelise.2 = (bf16[1024,128]{1,0:T(8,128)(2,1)S(1)}, bf16[1024,128]{1,0:T(8,128)(2,1)S(1)}, bf16[1024,128]{1,0:T(8,128)(2,1)S(1)}, bf16[1024,128]{1,0:T(8,128...) custom-call(s32[3]{0:T(128)S(1)} %pad_add_fusion.refs_0_, ...), custom_call_target="tpu_custom_call" | custom-call | flops 8999999488 | bytes 4194304 | tf_op jit(solution)/shard_map/channelise/pallas_call | solution.py:276
  80.3 13.3 %collective-permute-done.4.refs_3_ = bf16[2,16,8192]{2,1,0:T(8,128)(2,1)S(1)} collective-permute-done((bf16[2,16,8192]{2,1,0:T(8,128)(2,1)}, bf16[2,16,8192]{2,1,0:T(8,128)(2,1)S(1)}, u32[]{:S(2)}, u32[]{:S(2)}) %collective-permute-start.4) | collective-permute-done | bytes 524320 | tf_op jit(solution)/shard_map/ppermute | solution.py:483
  97.3 4.2 %collective-permute-start.10 = (bf16[32,2,16,128]{3,2,1,0:T(8,128)(2,1)S(1)}, bf16[32,2,16,128]{3,2,1,0:T(8,128)(2,1)S(1)}, u32[]{:S(2)}, u32[]{:S(2)}) collective-permute-start(bf16[32,2,16,128]{3,2,1,0:T(8,128)(2,1)S(1)} %bitcast.101), channel_id=1, source_target_pairs={{0,14},{2,8},{4,10},{6,12},{8,6},{10,0},{12,2},{14,4},{1,15},{3,9}... | collective-permute-start | bytes 786440 | tf_op jit(solution)/shard_map/ppermute | solution.py:483
  101.5 15.6 %channelise.3 = (bf16[4096,128]{1,0:T(8,128)(2,1)S(1)}, bf16[3072,128]{1,0:T(8,128)(2,1)S(1)}, bf16[1024,128]{1,0:T(8,128)(2,1)S(1)}) custom-call(s32[3]{0:T(128)S(1)} %pad_add_fusion.refs_0_, bf16[2,128,8192]{2,1,0:T(8,128)(2,1)S(1)} %bitcast.92, bf16[2,16,8192]{2,1,0:T(8,128)(2,1)S(1)} %collective-permute-done.3.refs_2_, ...), custom_call_target="tpu_custom_call" | custom-call | flops 8999999488 | bytes 4194304 | tf_op jit(solution)/shard_map/channelise/pallas_call | solution.py:276
  117.8 3.0 %collective-permute-start.13 = (bf16[32,2,16,128]{3,2,1,0:T(8,128)(2,1)S(1)}, bf16[32,2,16,128]{3,2,1,0:T(8,128)(2,1)S(1)}, u32[]{:S(2)}, u32[]{:S(2)}) collective-permute-start(bf16[32,2,16,128]{3,2,1,0:T(8,128)(2,1)S(1)} %bitcast.98), channel_id=1, source_target_pairs={{0,12},{2,14},{4,8},{6,10},{8,4},{10,6},{12,0},{14,2},{1,13},{3,15... | collective-permute-start | bytes 786440 | tf_op jit(solution)/shard_map/ppermute | solution.py:483
  120.8 3.1 %collective-permute-done.10 = bf16[32,2,16,128]{3,2,1,0:T(8,128)(2,1)S(1)} collective-permute-done((bf16[32,2,16,128]{3,2,1,0:T(8,128)(2,1)S(1)}, bf16[32,2,16,128]{3,2,1,0:T(8,128)(2,1)S(1)}, u32[]{:S(2)}, u32[]{:S(2)}) %collective-permute-start.10) | collective-permute-done | bytes 262176 | tf_op jit(solution)/shard_map/ppermute | solution.py:483
  125.1 4.2 %collective-permute-done.6 = bf16[32,2,16,128]{3,2,1,0:T(8,128)(2,1)S(1)} collective-permute-done((bf16[32,2,16,128]{3,2,1,0:T(8,128)(2,1)S(1)}, bf16[32,2,16,128]{3,2,1,0:T(8,128)(2,1)S(1)}, u32[]{:S(2)}, u32[]{:S(2)}) %collective-permute-start.6) | collective-permute-done | bytes 262176 | tf_op jit(solution)/shard_map/ppermute | solution.py:483
  129.4 21.7 %collective-permute-done.11 = bf16[96,2,16,128]{3,2,1,0:T(8,128)(2,1)S(1)} collective-permute-done((bf16[96,2,16,128]{3,2,1,0:T(8,128)(2,1)S(1)}, bf16[96,2,16,128]{3,2,1,0:T(8,128)(2,1)S(1)}, u32[]{:S(2)}, u32[]{:S(2)}) %collective-permute-start.11) | collective-permute-done | bytes 786464 | tf_op jit(solution)/shard_map/ppermute | solution.py:483
  152.1 2.1 collective-permute-start.14
  154.2 6.4 %collective-permute-done.15 = bf16[2,18,2,16,128]{4,3,2,1,0:T(8,128)(2,1)S(1)} collective-permute-done((bf16[2,18,2,16,128]{4,3,2,1,0:T(8,128)(2,1)S(1)}, bf16[2,18,2,16,128]{4,3,2,1,0:T(8,128)(2,1)S(1)}, u32[]{:S(2)}, u32[]{:S(2)}) %collective-permute-start.15) | collective-permute-done | bytes 294944 | tf_op jit(solution)/shard_map/ppermute | solution.py:483
  161.8 5.2 %collective-permute-done.17 = bf16[32,2,16,128]{3,2,1,0:T(8,128)(2,1)S(1)} collective-permute-done((bf16[32,2,16,128]{3,2,1,0:T(8,128)(2,1)S(1)}, bf16[32,2,16,128]{3,2,1,0:T(8,128)(2,1)S(1)}, u32[]{:S(2)}, u32[]{:S(2)}) %collective-permute-start.17) | collective-permute-done | bytes 262176 | tf_op jit(solution)/shard_map/ppermute | solution.py:483
  167.1 10.3 %collective-permute-done.14 = bf16[2,18,2,16,128]{4,3,2,1,0:T(8,128)(2,1)S(1)} collective-permute-done((bf16[2,18,2,16,128]{4,3,2,1,0:T(8,128)(2,1)S(1)}, bf16[2,18,2,16,128]{4,3,2,1,0:T(8,128)(2,1)S(1)}, u32[]{:S(2)}, u32[]{:S(2)}) %collective-permute-start.14) | collective-permute-done | bytes 294944 | tf_op jit(solution)/shard_map/ppermute | solution.py:483
  177.4 3.1 %collective-permute-done.21 = bf16[2,18,2,16,128]{4,3,2,1,0:T(8,128)(2,1)S(1)} collective-permute-done((bf16[2,18,2,16,128]{4,3,2,1,0:T(8,128)(2,1)S(1)}, bf16[2,18,2,16,128]{4,3,2,1,0:T(8,128)(2,1)S(1)}, u32[]{:S(2)}, u32[]{:S(2)}) %collective-permute-start.21) | collective-permute-done | bytes 294944 | tf_op jit(solution)/shard_map/ppermute | solution.py:483
  183.7 13.3 %correlate.2.refs_8_ = f32[8,32,2,2,64,128]{5,4,3,2,1,0:T(8,128)} custom-call(s32[3]{0:T(128)S(1)} %pad_add_fusion.refs_0_, bf16[512,256]{1,0:T(8,128)(2,1)S(1)} %fusion.1.refs_1_, bf16[2,256,512]{2,1,0:T(8,128)(2,1)S(1)} %fusion.refs_2_, f32[8,256]{1,0:T(8,128)S(1)} %tile.10.refs_3_, ...), custom_call_target="tpu_custom_call" | custom-call | flops 7312500224 | bytes 24772608 | tf_op jit(solution)/shard_map/correlate/pallas_call | solution.py:401
  197.0 4.2 %collective-permute-done.19 = bf16[2,14,2,16,128]{4,3,2,1,0:T(8,128)(2,1)S(1)} collective-permute-done((bf16[2,14,2,16,128]{4,3,2,1,0:T(8,128)(2,1)S(1)}, bf16[2,14,2,16,128]{4,3,2,1,0:T(8,128)(2,1)S(1)}, u32[]{:S(2)}, u32[]{:S(2)}) %collective-permute-start.19) | collective-permute-done | bytes 229408 | tf_op jit(solution)/shard_map/ppermute | solution.py:483
  203.2 2.1 collective-permute-done.23.refs_7_
  205.3 10.9 %correlate.3 = f32[8,32,2,2,64,128]{5,4,3,2,1,0:T(8,128)} custom-call(s32[3]{0:T(128)S(1)} %pad_add_fusion.refs_0_, bf16[512,256]{1,0:T(8,128)(2,1)S(1)} %fusion.1.refs_1_, bf16[2,256,512]{2,1,0:T(8,128)(2,1)S(1)} %fusion.refs_2_, f32[8,256]{1,0:T(8,128)S(1)} %tile.10.refs_3_, ...), custom_call_target="tpu_custom_call", output_to_operand_aliasing={{}: (8, {})} | custom-call | flops 5687499776 | bytes 19267584 | tf_op jit(solution)/shard_map/correlate/pallas_call | solution.py:401
  (91 shorter events, 19.2 us)
Async XLA Ops:
  1.1 12.8 %collective-permute-start = (bf16[2,16,8192]{2,1,0:T(8,128)(2,1)S(1)}, bf16[2,16,8192]{2,1,0:T(8,128)(2,1)S(1)}, u32[]{:S(2)}, u32[]{:S(2)}) collective-permute-start(bf16[2,16,8192]{2,1,0:T(8,128)(2,1)S(1)} %dynamic-slice_bitcast_fusion), channel_id=1, source_target_pairs={{0,2},{2,4},{4,6},{6,0},{8,10},{10,12},{12,14},{14,8},{1,3},{3,5},... | collective-permute-start | bytes 1572872 | tf_op jit(solution)/shard_map/ppermute | solution.py:483
  5.5 41.3 %collective-permute-start.1 = (bf16[2,16,8192]{2,1,0:T(8,128)(2,1)S(1)}, bf16[2,16,8192]{2,1,0:T(8,128)(2,1)S(1)}, u32[]{:S(2)}, u32[]{:S(2)}) collective-permute-start(bf16[2,16,8192]{2,1,0:T(8,128)(2,1)S(1)} %get-tuple-element.117), channel_id=1, source_target_pairs={{0,4},{2,6},{4,0},{6,2},{8,12},{10,14},{12,8},{14,10},{1,5},{3,7},... | collective-permute-start | bytes 1572872 | tf_op jit(solution)/shard_map/ppermute | solution.py:483
  13.9 33.3 %collective-permute-start.2 = (bf16[2,16,8192]{2,1,0:T(8,128)(2,1)}, bf16[2,16,8192]{2,1,0:T(8,128)(2,1)S(1)}, u32[]{:S(2)}, u32[]{:S(2)}) collective-permute-start(bf16[2,16,8192]{2,1,0:T(8,128)(2,1)} %get-tuple-element.64), channel_id=1, source_target_pairs={{0,6},{2,0},{4,2},{6,4},{8,14},{10,8},{12,10},{14,12},{1,7},{3,1},... | collective-permute-start | bytes 1572872 | tf_op jit(solution)/shard_map/ppermute | solution.py:483
  46.7 11.7 %collective-permute-start.3 = (bf16[2,16,8192]{2,1,0:T(8,128)(2,1)}, bf16[2,16,8192]{2,1,0:T(8,128)(2,1)S(1)}, u32[]{:S(2)}, u32[]{:S(2)}) collective-permute-start(bf16[2,16,8192]{2,1,0:T(8,128)(2,1)} %get-tuple-element.70), channel_id=1, source_target_pairs={{0,2},{2,4},{4,6},{6,0},{8,10},{10,12},{12,14},{14,8},{1,3},{3,5},... | collective-permute-start | bytes 1572872 | tf_op jit(solution)/shard_map/ppermute | solution.py:483
  47.3 54.2 %collective-permute-start.5 = (bf16[2,16,8192]{2,1,0:T(8,128)(2,1)S(1)}, bf16[2,16,8192]{2,1,0:T(8,128)(2,1)S(1)}, u32[]{:S(2)}, u32[]{:S(2)}) collective-permute-start(bf16[2,16,8192]{2,1,0:T(8,128)(2,1)S(1)} %get-tuple-element.81), channel_id=1, source_target_pairs={{0,6},{2,0},{4,2},{6,4},{8,14},{10,8},{12,10},{14,12},{1,7},{3,1},... | collective-permute-start | bytes 1572872 | tf_op jit(solution)/shard_map/ppermute | solution.py:483
  58.4 35.2 %collective-permute-start.4 = (bf16[2,16,8192]{2,1,0:T(8,128)(2,1)}, bf16[2,16,8192]{2,1,0:T(8,128)(2,1)S(1)}, u32[]{:S(2)}, u32[]{:S(2)}) collective-permute-start(bf16[2,16,8192]{2,1,0:T(8,128)(2,1)} %get-tuple-element.71), channel_id=1, source_target_pairs={{0,4},{2,6},{4,0},{6,2},{8,12},{10,14},{12,8},{14,10},{1,5},{3,7},... | collective-permute-start | bytes 1572872 | tf_op jit(solution)/shard_map/ppermute | solution.py:483
  93.6 23.8 %collective-permute-start.7 = (bf16[32,2,16,128]{3,2,1,0:T(8,128)(2,1)S(1)}, bf16[32,2,16,128]{3,2,1,0:T(8,128)(2,1)S(1)}, u32[]{:S(2)}, u32[]{:S(2)}) collective-permute-start(bf16[32,2,16,128]{3,2,1,0:T(8,128)(2,1)S(1)} %bitcast.104), channel_id=1, source_target_pairs={{0,2},{2,4},{4,6},{6,0},{8,10},{10,12},{12,14},{14,8},{1,3},{3,5},... | collective-permute-start | bytes 786440 | tf_op jit(solution)/shard_map/ppermute | solution.py:483
  95.5 22.3 %collective-permute-start.8 = (bf16[32,2,16,128]{3,2,1,0:T(8,128)(2,1)S(1)}, bf16[32,2,16,128]{3,2,1,0:T(8,128)(2,1)S(1)}, u32[]{:S(2)}, u32[]{:S(2)}) collective-permute-start(bf16[32,2,16,128]{3,2,1,0:T(8,128)(2,1)S(1)} %bitcast.103), channel_id=1, source_target_pairs={{0,10},{2,12},{4,14},{6,8},{8,2},{10,4},{12,6},{14,0},{1,11},{3,13... | collective-permute-start | bytes 786440 | tf_op jit(solution)/shard_map/ppermute | solution.py:483
  96.9 23.9 %collective-permute-start.9 = (bf16[32,2,16,128]{3,2,1,0:T(8,128)(2,1)S(1)}, bf16[32,2,16,128]{3,2,1,0:T(8,128)(2,1)S(1)}, u32[]{:S(2)}, u32[]{:S(2)}) collective-permute-start(bf16[32,2,16,128]{3,2,1,0:T(8,128)(2,1)S(1)} %bitcast.102), channel_id=1, source_target_pairs={{0,6},{2,0},{4,2},{6,4},{8,14},{10,8},{12,10},{14,12},{1,7},{3,1},... | collective-permute-start | bytes 786440 | tf_op jit(solution)/shard_map/ppermute | solution.py:483
  97.3 26.5 %collective-permute-start.10 = (bf16[32,2,16,128]{3,2,1,0:T(8,128)(2,1)S(1)}, bf16[32,2,16,128]{3,2,1,0:T(8,128)(2,1)S(1)}, u32[]{:S(2)}, u32[]{:S(2)}) collective-permute-start(bf16[32,2,16,128]{3,2,1,0:T(8,128)(2,1)S(1)} %bitcast.101), channel_id=1, source_target_pairs={{0,14},{2,8},{4,10},{6,12},{8,6},{10,0},{12,2},{14,4},{1,15},{3,9}... | collective-permute-start | bytes 786440 | tf_op jit(solution)/shard_map/ppermute | solution.py:483
  117.0 12.2 %collective-permute-start.6 = (bf16[32,2,16,128]{3,2,1,0:T(8,128)(2,1)S(1)}, bf16[32,2,16,128]{3,2,1,0:T(8,128)(2,1)S(1)}, u32[]{:S(2)}, u32[]{:S(2)}) collective-permute-start(bf16[32,2,16,128]{3,2,1,0:T(8,128)(2,1)S(1)} %bitcast.100), channel_id=1, source_target_pairs={{0,8},{2,10},{4,12},{6,14},{8,0},{10,2},{12,4},{14,6},{1,9},{3,11}... | collective-permute-start | bytes 786440 | tf_op jit(solution)/shard_map/ppermute | solution.py:483
  117.4 33.8 %collective-permute-start.12 = (bf16[32,2,16,128]{3,2,1,0:T(8,128)(2,1)S(1)}, bf16[32,2,16,128]{3,2,1,0:T(8,128)(2,1)S(1)}, u32[]{:S(2)}, u32[]{:S(2)}) collective-permute-start(bf16[32,2,16,128]{3,2,1,0:T(8,128)(2,1)S(1)} %bitcast.99), channel_id=1, source_target_pairs={{0,4},{2,6},{4,0},{6,2},{8,12},{10,14},{12,8},{14,10},{1,5},{3,7},... | collective-permute-start | bytes 786440 | tf_op jit(solution)/shard_map/ppermute | solution.py:483
  117.8 33.6 %collective-permute-start.13 = (bf16[32,2,16,128]{3,2,1,0:T(8,128)(2,1)S(1)}, bf16[32,2,16,128]{3,2,1,0:T(8,128)(2,1)S(1)}, u32[]{:S(2)}, u32[]{:S(2)}) collective-permute-start(bf16[32,2,16,128]{3,2,1,0:T(8,128)(2,1)S(1)} %bitcast.98), channel_id=1, source_target_pairs={{0,12},{2,14},{4,8},{6,10},{8,4},{10,6},{12,0},{14,2},{1,13},{3,15... | collective-permute-start | bytes 786440 | tf_op jit(solution)/shard_map/ppermute | solution.py:483
  123.9 27.3 %collective-permute-start.11 = (bf16[96,2,16,128]{3,2,1,0:T(8,128)(2,1)S(1)}, bf16[96,2,16,128]{3,2,1,0:T(8,128)(2,1)S(1)}, u32[]{:S(2)}, u32[]{:S(2)}) collective-permute-start(bf16[96,2,16,128]{3,2,1,0:T(8,128)(2,1)S(1)} %bitcast.96), channel_id=1, source_target_pairs={{0,8},{2,10},{4,12},{6,14},{8,0},{10,2},{12,4},{14,6},{1,9},{3,11}... | collective-permute-start | bytes 2359304 | tf_op jit(solution)/shard_map/ppermute | solution.py:483
  151.5 26.0 %collective-permute-start.16 = (bf16[8,32,2,16,128]{4,3,2,1,0:T(8,128)(2,1)S(1)}, bf16[8,32,2,16,128]{4,3,2,1,0:T(8,128)(2,1)S(1)}, u32[]{:S(2)}, u32[]{:S(2)}) collective-permute-start(bf16[8,32,2,16,128]{4,3,2,1,0:T(8,128)(2,1)S(1)} %bitcast_dynamic-update-slice_fusion.refs_4_), channel_id=1, source_target_pairs={{0,1},{1,0},{2,3},{3,2},{4,5},{5,4},{6,7},{7,6},{8,9},{9,8},{10,11... | collective-permute-start | bytes 6291464 | tf_op jit(solution)/shard_map/ppermute | solution.py:483
  152.0 8.6 %collective-permute-start.15 = (bf16[2,18,2,16,128]{4,3,2,1,0:T(8,128)(2,1)S(1)}, bf16[2,18,2,16,128]{4,3,2,1,0:T(8,128)(2,1)S(1)}, u32[]{:S(2)}, u32[]{:S(2)}) collective-permute-start(bf16[2,18,2,16,128]{4,3,2,1,0:T(8,128)(2,1)S(1)} %pad_maximum_fusion.3), channel_id=1, source_target_pairs={{0,2},{2,4},{4,6},{6,0},{8,10},{10,12},{12,14},{14,8},{1,3},{3,5},... | collective-permute-start | bytes 884744 | tf_op jit(solution)/shard_map/ppermute | solution.py:483
  152.1 25.4 %collective-permute-start.14 = (bf16[2,18,2,16,128]{4,3,2,1,0:T(8,128)(2,1)S(1)}, bf16[2,18,2,16,128]{4,3,2,1,0:T(8,128)(2,1)S(1)}, u32[]{:S(2)}, u32[]{:S(2)}) collective-permute-start(bf16[2,18,2,16,128]{4,3,2,1,0:T(8,128)(2,1)S(1)} %pad_maximum_fusion.2), channel_id=1, source_target_pairs={{0,4},{2,6},{4,0},{6,2},{8,12},{10,14},{12,8},{14,10},{1,5},{3,7},... | collective-permute-start | bytes 884744 | tf_op jit(solution)/shard_map/ppermute | solution.py:483
  154.1 26.4 %collective-permute-start.21 = (bf16[2,18,2,16,128]{4,3,2,1,0:T(8,128)(2,1)S(1)}, bf16[2,18,2,16,128]{4,3,2,1,0:T(8,128)(2,1)S(1)}, u32[]{:S(2)}, u32[]{:S(2)}) collective-permute-start(bf16[2,18,2,16,128]{4,3,2,1,0:T(8,128)(2,1)S(1)} %pad_maximum_fusion.4), channel_id=1, source_target_pairs={{0,6},{2,0},{4,2},{6,4},{8,14},{10,8},{12,10},{14,12},{1,7},{3,1},... | collective-permute-start | bytes 884744 | tf_op jit(solution)/shard_map/ppermute | solution.py:483
  160.6 6.5 %collective-permute-start.17 = (bf16[32,2,16,128]{3,2,1,0:T(8,128)(2,1)S(1)}, bf16[32,2,16,128]{3,2,1,0:T(8,128)(2,1)S(1)}, u32[]{:S(2)}, u32[]{:S(2)}) collective-permute-start(bf16[32,2,16,128]{3,2,1,0:T(8,128)(2,1)S(1)} %bitcast.97), channel_id=1, source_target_pairs={{0,8},{2,10},{4,12},{6,14},{8,0},{10,2},{12,4},{14,6},{1,9},{3,11}... | collective-permute-start | bytes 786440 | tf_op jit(solution)/shard_map/ppermute | solution.py:483
  180.7 3.0 %collective-permute-start.22 = (bf16[8,18,2,16,128]{4,3,2,1,0:T(8,128)(2,1)S(1)}, bf16[8,18,2,16,128]{4,3,2,1,0:T(8,128)(2,1)S(1)}, u32[]{:S(2)}, u32[]{:S(2)}) collective-permute-start(bf16[8,18,2,16,128]{4,3,2,1,0:T(8,128)(2,1)S(1)} %bitcast.86), channel_id=1, source_target_pairs={{0,1},{1,0},{2,3},{3,2},{4,5},{5,4},{6,7},{7,6},{8,9},{9,8},{10,11... | collective-permute-start | bytes 3538952 | tf_op jit(solution)/shard_map/ppermute | solution.py:483
  181.2 15.8 %collective-permute-start.18 = (bf16[2,14,2,16,128]{4,3,2,1,0:T(8,128)(2,1)S(1)}, bf16[2,14,2,16,128]{4,3,2,1,0:T(8,128)(2,1)S(1)}, u32[]{:S(2)}, u32[]{:S(2)}) collective-permute-start(bf16[2,14,2,16,128]{4,3,2,1,0:T(8,128)(2,1)S(1)} %pad_maximum_fusion.5), channel_id=1, source_target_pairs={{0,2},{2,4},{4,6},{6,0},{8,10},{10,12},{12,14},{14,8},{1,3},{3,5},... | collective-permute-start | bytes 688136 | tf_op jit(solution)/shard_map/ppermute | solution.py:483
  181.3 19.9 %collective-permute-start.19 = (bf16[2,14,2,16,128]{4,3,2,1,0:T(8,128)(2,1)S(1)}, bf16[2,14,2,16,128]{4,3,2,1,0:T(8,128)(2,1)S(1)}, u32[]{:S(2)}, u32[]{:S(2)}) collective-permute-start(bf16[2,14,2,16,128]{4,3,2,1,0:T(8,128)(2,1)S(1)} %pad_maximum_fusion.6), channel_id=1, source_target_pairs={{0,4},{2,6},{4,0},{6,2},{8,12},{10,14},{12,8},{14,10},{1,5},{3,7},... | collective-permute-start | bytes 688136 | tf_op jit(solution)/shard_map/ppermute | solution.py:483
  181.7 20.8 %collective-permute-start.20 = (bf16[2,14,2,16,128]{4,3,2,1,0:T(8,128)(2,1)S(1)}, bf16[2,14,2,16,128]{4,3,2,1,0:T(8,128)(2,1)S(1)}, u32[]{:S(2)}, u32[]{:S(2)}) collective-permute-start(bf16[2,14,2,16,128]{4,3,2,1,0:T(8,128)(2,1)S(1)} %pad_maximum_fusion.7), channel_id=1, source_target_pairs={{0,6},{2,0},{4,2},{6,4},{8,14},{10,8},{12,10},{14,12},{1,7},{3,1},... | collective-permute-start | bytes 688136 | tf_op jit(solution)/shard_map/ppermute | solution.py:483
  202.6 2.6 %collective-permute-start.23 = (bf16[8,14,2,16,128]{4,3,2,1,0:T(8,128)(2,1)S(1)}, bf16[8,14,2,16,128]{4,3,2,1,0:T(8,128)(2,1)S(1)}, u32[]{:S(2)}, u32[]{:S(2)}) collective-permute-start(bf16[8,14,2,16,128]{4,3,2,1,0:T(8,128)(2,1)S(1)} %bitcast.88), channel_id=1, source_target_pairs={{0,1},{1,0},{2,3},{3,2},{4,5},{5,4},{6,7},{7,6},{8,9},{9,8},{10,11... | collective-permute-start | bytes 2752520 | tf_op jit(solution)/shard_map/ppermute | solution.py:483
  (8 other events, 200.0 us)

commit v2 on v1

--- a/solution.py
+++ b/solution.py
@@ -346,14 +346,14 @@
                     right_sel_ref[pol],
                     (((0,), (0,)), ((), ())),
                     preferred_element_type=jnp.float32,
-                )
+                ).astype(jnp.bfloat16)
             )
         for pair in range(tiles // 2):
             first, second = (v[:, pair * 2 * width : (pair + 1) * 2 * width] for v in right)
             even = jnp.where(lower, first, second)
             odd = pltpu.roll(jnp.where(lower, second, first), width, 1)
-            right_ref[2 * pair] = even.astype(jnp.bfloat16)
-            right_ref[2 * pair + 1] = odd.astype(jnp.bfloat16)
+            right_ref[2 * pair] = even
+            right_ref[2 * pair + 1] = odd
 
     def multiply(number, left_ref, right_ref):
         for tile in range(tiles):
@@ -500,7 +500,7 @@
     def columns(near, far):
         return jnp.stack([near, far])
 
-    cut = bands * 9 // 16
+    cut = bands * 5 // 8
     rest = bands - cut
     pairs = [(x, z) for z in range(time_count) for x in range(chan_count)]
     early_pairs = [(x, z) for z in (1, 3) for x in range(2)]

time: 217 us -> 216 us (level)
  transfers between devices with their start and end apart: 24 -> 24, of which waited for: 15 -> 14; matrix products, arithmetic and copies ran while one was open for 2% -> 2% of each run, Pallas kernels for 21% -> 21%
where the time goes in v2:
time: 216 us; the launch traced here: 215 us
  waiting for transfers between devices  121 us (56%)
  Pallas kernels  55.4 us (26%)
  starting transfers between devices  29.6 us (14%)
  local copies, waits for them, and re-layouts  7.09 us (3%)
    ppermute x24, waiting for transfers between devices, travel(): return lax.ppermute(value, axes, pairs)  121 us
    pallas_call x2, Pallas kernels, channelise(): pl.pallas_call(lambda *refs: channelise_kernel(frames, chunk, columns, pl...  31.1 us
    ppermute x24, starting transfers between devices, travel(): return lax.ppermute(value, axes, pairs)  29.6 us
    pallas_call x2, Pallas kernels, correlate_tiles(): pl.pallas_call(lambda *refs: correlate_kernel(starts, width, *refs), grid...  24.3 us
  transfers between devices with their start and end apart: 24, of which 14 were waited for; matrix products, arithmetic and copies ran while one was open for 2% of the time, Pallas kernels for 21%

profile of v2, /device:TPU:11, one launch (start us, length us, event | category | flops | bytes accessed | tf_op | source)
XLA Modules:
  0.0 214.8 jit_solution(332226422193569251)
XLA Ops:
  2.5 3.0 %constant_dynamic-slice_fusion = (bf16[2,16,8192]{2,1,0:T(8,128)(2,1)}, bf16[2,16,8192]{2,1,0:T(8,128)(2,1)S(1)}, bf16[2,16,8192]{2,1,0:T(8,128)(2,1)S(1)}, bf16[2,16,8192]{2,1,0:T(8,128)(2,1)}, bf16[2,16,8192]{2,1,0:T(8,128)(2,1)}) fusion(bf16[2,128,8192]{2,1,0:T(8,128)(2,1)} %bitcast.90, s32[]{:T(128)S(6)} %select_n.109, s32[]{:T(128)S(6)} %select_n.108, ...), kind=kLoop, calls=%fused_computation.137 | loop fusion | bytes 5242900 | tf_op jit(solution)/shard_map/dynamic_slice | solution.py:490
  7.3 6.6 %collective-permute-done.refs_2_ = bf16[2,16,8192]{2,1,0:T(8,128)(2,1)S(1)} collective-permute-done((bf16[2,16,8192]{2,1,0:T(8,128)(2,1)S(1)}, bf16[2,16,8192]{2,1,0:T(8,128)(2,1)S(1)}, u32[]{:S(2)}, u32[]{:S(2)}) %collective-permute-start) | collective-permute-done | bytes 524320 | tf_op jit(solution)/shard_map/ppermute | solution.py:483
  13.9 2.1 collective-permute-start.2
  16.1 30.7 %collective-permute-done.1.refs_3_ = bf16[2,16,8192]{2,1,0:T(8,128)(2,1)S(1)} collective-permute-done((bf16[2,16,8192]{2,1,0:T(8,128)(2,1)S(1)}, bf16[2,16,8192]{2,1,0:T(8,128)(2,1)S(1)}, u32[]{:S(2)}, u32[]{:S(2)}) %collective-permute-start.1) | collective-permute-done | bytes 524320 | tf_op jit(solution)/shard_map/ppermute | solution.py:483
  48.8 9.7 %collective-permute-done.3.refs_2_ = bf16[2,16,8192]{2,1,0:T(8,128)(2,1)S(1)} collective-permute-done((bf16[2,16,8192]{2,1,0:T(8,128)(2,1)}, bf16[2,16,8192]{2,1,0:T(8,128)(2,1)S(1)}, u32[]{:S(2)}, u32[]{:S(2)}) %collective-permute-start.3) | collective-permute-done | bytes 524320 | tf_op jit(solution)/shard_map/ppermute | solution.py:483
  58.4 4.1 %collective-permute-start.4 = (bf16[2,16,8192]{2,1,0:T(8,128)(2,1)}, bf16[2,16,8192]{2,1,0:T(8,128)(2,1)S(1)}, u32[]{:S(2)}, u32[]{:S(2)}) collective-permute-start(bf16[2,16,8192]{2,1,0:T(8,128)(2,1)} %get-tuple-element.71), channel_id=1, source_target_pairs={{0,4},{2,6},{4,0},{6,2},{8,12},{10,14},{12,8},{14,10},{1,5},{3,7},... | collective-permute-start | bytes 1572872 | tf_op jit(solution)/shard_map/ppermute | solution.py:483
  62.6 2.2 %copy-done = bf16[2,1,128,8192]{3,2,1,0:T(8,128)(2,1)S(1)} copy-done((bf16[2,1,128,8192]{3,2,1,0:T(8,128)(2,1)S(1)}, bf16[2,1,128,8192]{3,2,1,0:T(8,128)(2,1)}, u32[]{:S(2)}) %copy-start) | copy-done | bytes 4194328
  64.8 15.6 %channelise.2 = (bf16[1024,128]{1,0:T(8,128)(2,1)S(1)}, bf16[1024,128]{1,0:T(8,128)(2,1)S(1)}, bf16[1024,128]{1,0:T(8,128)(2,1)S(1)}, bf16[1024,128]{1,0:T(8,128...) custom-call(s32[3]{0:T(128)S(1)} %pad_add_fusion.refs_0_, ...), custom_call_target="tpu_custom_call" | custom-call | flops 8999999488 | bytes 4194304 | tf_op jit(solution)/shard_map/channelise/pallas_call | solution.py:276
  80.3 13.3 %collective-permute-done.4.refs_3_ = bf16[2,16,8192]{2,1,0:T(8,128)(2,1)S(1)} collective-permute-done((bf16[2,16,8192]{2,1,0:T(8,128)(2,1)}, bf16[2,16,8192]{2,1,0:T(8,128)(2,1)S(1)}, u32[]{:S(2)}, u32[]{:S(2)}) %collective-permute-start.4) | collective-permute-done | bytes 524320 | tf_op jit(solution)/shard_map/ppermute | solution.py:483
  93.6 1.9 collective-permute-start.7
  97.3 4.2 %collective-permute-start.10 = (bf16[32,2,16,128]{3,2,1,0:T(8,128)(2,1)S(1)}, bf16[32,2,16,128]{3,2,1,0:T(8,128)(2,1)S(1)}, u32[]{:S(2)}, u32[]{:S(2)}) collective-permute-start(bf16[32,2,16,128]{3,2,1,0:T(8,128)(2,1)S(1)} %bitcast.101), channel_id=1, source_target_pairs={{0,14},{2,8},{4,10},{6,12},{8,6},{10,0},{12,2},{14,4},{1,15},{3,9}... | collective-permute-start | bytes 786440 | tf_op jit(solution)/shard_map/ppermute | solution.py:483
  101.5 15.6 %channelise.3 = (bf16[4096,128]{1,0:T(8,128)(2,1)S(1)}, bf16[3072,128]{1,0:T(8,128)(2,1)S(1)}, bf16[1024,128]{1,0:T(8,128)(2,1)S(1)}) custom-call(s32[3]{0:T(128)S(1)} %pad_add_fusion.refs_0_, bf16[2,128,8192]{2,1,0:T(8,128)(2,1)S(1)} %bitcast.92, bf16[2,16,8192]{2,1,0:T(8,128)(2,1)S(1)} %collective-permute-done.3.refs_2_, ...), custom_call_target="tpu_custom_call" | custom-call | flops 8999999488 | bytes 4194304 | tf_op jit(solution)/shard_map/channelise/pallas_call | solution.py:276
  117.8 3.0 %collective-permute-start.13 = (bf16[32,2,16,128]{3,2,1,0:T(8,128)(2,1)S(1)}, bf16[32,2,16,128]{3,2,1,0:T(8,128)(2,1)S(1)}, u32[]{:S(2)}, u32[]{:S(2)}) collective-permute-start(bf16[32,2,16,128]{3,2,1,0:T(8,128)(2,1)S(1)} %bitcast.98), channel_id=1, source_target_pairs={{0,12},{2,14},{4,8},{6,10},{8,4},{10,6},{12,0},{14,2},{1,13},{3,15... | collective-permute-start | bytes 786440 | tf_op jit(solution)/shard_map/ppermute | solution.py:483
  120.8 3.1 %collective-permute-done.10 = bf16[32,2,16,128]{3,2,1,0:T(8,128)(2,1)S(1)} collective-permute-done((bf16[32,2,16,128]{3,2,1,0:T(8,128)(2,1)S(1)}, bf16[32,2,16,128]{3,2,1,0:T(8,128)(2,1)S(1)}, u32[]{:S(2)}, u32[]{:S(2)}) %collective-permute-start.10) | collective-permute-done | bytes 262176 | tf_op jit(solution)/shard_map/ppermute | solution.py:483
  125.1 4.2 %collective-permute-done.6 = bf16[32,2,16,128]{3,2,1,0:T(8,128)(2,1)S(1)} collective-permute-done((bf16[32,2,16,128]{3,2,1,0:T(8,128)(2,1)S(1)}, bf16[32,2,16,128]{3,2,1,0:T(8,128)(2,1)S(1)}, u32[]{:S(2)}, u32[]{:S(2)}) %collective-permute-start.6) | collective-permute-done | bytes 262176 | tf_op jit(solution)/shard_map/ppermute | solution.py:483
  129.4 21.7 %collective-permute-done.11 = bf16[96,2,16,128]{3,2,1,0:T(8,128)(2,1)S(1)} collective-permute-done((bf16[96,2,16,128]{3,2,1,0:T(8,128)(2,1)S(1)}, bf16[96,2,16,128]{3,2,1,0:T(8,128)(2,1)S(1)}, u32[]{:S(2)}, u32[]{:S(2)}) %collective-permute-start.11) | collective-permute-done | bytes 786464 | tf_op jit(solution)/shard_map/ppermute | solution.py:483
  152.1 2.1 collective-permute-start.14
  154.2 7.2 %collective-permute-done.15 = bf16[2,20,2,16,128]{4,3,2,1,0:T(8,128)(2,1)S(1)} collective-permute-done((bf16[2,20,2,16,128]{4,3,2,1,0:T(8,128)(2,1)S(1)}, bf16[2,20,2,16,128]{4,3,2,1,0:T(8,128)(2,1)S(1)}, u32[]{:S(2)}, u32[]{:S(2)}) %collective-permute-start.15) | collective-permute-done | bytes 327712 | tf_op jit(solution)/shard_map/ppermute | solution.py:483
  162.6 5.3 %collective-permute-done.17 = bf16[32,2,16,128]{3,2,1,0:T(8,128)(2,1)S(1)} collective-permute-done((bf16[32,2,16,128]{3,2,1,0:T(8,128)(2,1)S(1)}, bf16[32,2,16,128]{3,2,1,0:T(8,128)(2,1)S(1)}, u32[]{:S(2)}, u32[]{:S(2)}) %collective-permute-start.17) | collective-permute-done | bytes 262176 | tf_op jit(solution)/shard_map/ppermute | solution.py:483
  167.9 12.4 %collective-permute-done.14 = bf16[2,20,2,16,128]{4,3,2,1,0:T(8,128)(2,1)S(1)} collective-permute-done((bf16[2,20,2,16,128]{4,3,2,1,0:T(8,128)(2,1)S(1)}, bf16[2,20,2,16,128]{4,3,2,1,0:T(8,128)(2,1)S(1)}, u32[]{:S(2)}, u32[]{:S(2)}) %collective-permute-start.14) | collective-permute-done | bytes 327712 | tf_op jit(solution)/shard_map/ppermute | solution.py:483
  180.2 3.1 %collective-permute-done.21 = bf16[2,20,2,16,128]{4,3,2,1,0:T(8,128)(2,1)S(1)} collective-permute-done((bf16[2,20,2,16,128]{4,3,2,1,0:T(8,128)(2,1)S(1)}, bf16[2,20,2,16,128]{4,3,2,1,0:T(8,128)(2,1)S(1)}, u32[]{:S(2)}, u32[]{:S(2)}) %collective-permute-start.21) | collective-permute-done | bytes 327712 | tf_op jit(solution)/shard_map/ppermute | solution.py:483
  186.7 14.6 %correlate.2.refs_8_ = f32[8,32,2,2,64,128]{5,4,3,2,1,0:T(8,128)} custom-call(s32[3]{0:T(128)S(1)} %pad_add_fusion.refs_0_, bf16[512,256]{1,0:T(8,128)(2,1)S(1)} %fusion.1.refs_1_, bf16[2,256,512]{2,1,0:T(8,128)(2,1)S(1)} %fusion.refs_2_, f32[8,256]{1,0:T(8,128)S(1)} %tile.10.refs_3_, ...), custom_call_target="tpu_custom_call" | custom-call | flops 8125000192 | bytes 27525120 | tf_op jit(solution)/shard_map/correlate/pallas_call | solution.py:401
  203.2 1.9 collective-permute-done.23.refs_7_
  205.1 9.7 %correlate.3 = f32[8,32,2,2,64,128]{5,4,3,2,1,0:T(8,128)} custom-call(s32[3]{0:T(128)S(1)} %pad_add_fusion.refs_0_, bf16[512,256]{1,0:T(8,128)(2,1)S(1)} %fusion.1.refs_1_, bf16[2,256,512]{2,1,0:T(8,128)(2,1)S(1)} %fusion.refs_2_, f32[8,256]{1,0:T(8,128)S(1)} %tile.10.refs_3_, ...), custom_call_target="tpu_custom_call", output_to_operand_aliasing={{}: (8, {})} | custom-call | flops 4874999808 | bytes 16515072 | tf_op jit(solution)/shard_map/correlate/pallas_call | solution.py:401
  (91 shorter events, 17.5 us)
Async XLA Ops:
  1.1 12.8 %collective-permute-start = (bf16[2,16,8192]{2,1,0:T(8,128)(2,1)S(1)}, bf16[2,16,8192]{2,1,0:T(8,128)(2,1)S(1)}, u32[]{:S(2)}, u32[]{:S(2)}) collective-permute-start(bf16[2,16,8192]{2,1,0:T(8,128)(2,1)S(1)} %dynamic-slice_bitcast_fusion), channel_id=1, source_target_pairs={{0,2},{2,4},{4,6},{6,0},{8,10},{10,12},{12,14},{14,8},{1,3},{3,5},... | collective-permute-start | bytes 1572872 | tf_op jit(solution)/shard_map/ppermute | solution.py:483
  5.5 41.3 %collective-permute-start.1 = (bf16[2,16,8192]{2,1,0:T(8,128)(2,1)S(1)}, bf16[2,16,8192]{2,1,0:T(8,128)(2,1)S(1)}, u32[]{:S(2)}, u32[]{:S(2)}) collective-permute-start(bf16[2,16,8192]{2,1,0:T(8,128)(2,1)S(1)} %get-tuple-element.117), channel_id=1, source_target_pairs={{0,4},{2,6},{4,0},{6,2},{8,12},{10,14},{12,8},{14,10},{1,5},{3,7},... | collective-permute-start | bytes 1572872 | tf_op jit(solution)/shard_map/ppermute | solution.py:483
  13.9 33.3 %collective-permute-start.2 = (bf16[2,16,8192]{2,1,0:T(8,128)(2,1)}, bf16[2,16,8192]{2,1,0:T(8,128)(2,1)S(1)}, u32[]{:S(2)}, u32[]{:S(2)}) collective-permute-start(bf16[2,16,8192]{2,1,0:T(8,128)(2,1)} %get-tuple-element.64), channel_id=1, source_target_pairs={{0,6},{2,0},{4,2},{6,4},{8,14},{10,8},{12,10},{14,12},{1,7},{3,1},... | collective-permute-start | bytes 1572872 | tf_op jit(solution)/shard_map/ppermute | solution.py:483
  46.7 11.7 %collective-permute-start.3 = (bf16[2,16,8192]{2,1,0:T(8,128)(2,1)}, bf16[2,16,8192]{2,1,0:T(8,128)(2,1)S(1)}, u32[]{:S(2)}, u32[]{:S(2)}) collective-permute-start(bf16[2,16,8192]{2,1,0:T(8,128)(2,1)} %get-tuple-element.70), channel_id=1, source_target_pairs={{0,2},{2,4},{4,6},{6,0},{8,10},{10,12},{12,14},{14,8},{1,3},{3,5},... | collective-permute-start | bytes 1572872 | tf_op jit(solution)/shard_map/ppermute | solution.py:483
  47.3 54.2 %collective-permute-start.5 = (bf16[2,16,8192]{2,1,0:T(8,128)(2,1)S(1)}, bf16[2,16,8192]{2,1,0:T(8,128)(2,1)S(1)}, u32[]{:S(2)}, u32[]{:S(2)}) collective-permute-start(bf16[2,16,8192]{2,1,0:T(8,128)(2,1)S(1)} %get-tuple-element.81), channel_id=1, source_target_pairs={{0,6},{2,0},{4,2},{6,4},{8,14},{10,8},{12,10},{14,12},{1,7},{3,1},... | collective-permute-start | bytes 1572872 | tf_op jit(solution)/shard_map/ppermute | solution.py:483
  58.4 35.2 %collective-permute-start.4 = (bf16[2,16,8192]{2,1,0:T(8,128)(2,1)}, bf16[2,16,8192]{2,1,0:T(8,128)(2,1)S(1)}, u32[]{:S(2)}, u32[]{:S(2)}) collective-permute-start(bf16[2,16,8192]{2,1,0:T(8,128)(2,1)} %get-tuple-element.71), channel_id=1, source_target_pairs={{0,4},{2,6},{4,0},{6,2},{8,12},{10,14},{12,8},{14,10},{1,5},{3,7},... | collective-permute-start | bytes 1572872 | tf_op jit(solution)/shard_map/ppermute | solution.py:483
  93.6 23.8 %collective-permute-start.7 = (bf16[32,2,16,128]{3,2,1,0:T(8,128)(2,1)S(1)}, bf16[32,2,16,128]{3,2,1,0:T(8,128)(2,1)S(1)}, u32[]{:S(2)}, u32[]{:S(2)}) collective-permute-start(bf16[32,2,16,128]{3,2,1,0:T(8,128)(2,1)S(1)} %bitcast.104), channel_id=1, source_target_pairs={{0,2},{2,4},{4,6},{6,0},{8,10},{10,12},{12,14},{14,8},{1,3},{3,5},... | collective-permute-start | bytes 786440 | tf_op jit(solution)/shard_map/ppermute | solution.py:483
  95.5 22.3 %collective-permute-start.8 = (bf16[32,2,16,128]{3,2,1,0:T(8,128)(2,1)S(1)}, bf16[32,2,16,128]{3,2,1,0:T(8,128)(2,1)S(1)}, u32[]{:S(2)}, u32[]{:S(2)}) collective-permute-start(bf16[32,2,16,128]{3,2,1,0:T(8,128)(2,1)S(1)} %bitcast.103), channel_id=1, source_target_pairs={{0,10},{2,12},{4,14},{6,8},{8,2},{10,4},{12,6},{14,0},{1,11},{3,13... | collective-permute-start | bytes 786440 | tf_op jit(solution)/shard_map/ppermute | solution.py:483
  96.9 23.9 %collective-permute-start.9 = (bf16[32,2,16,128]{3,2,1,0:T(8,128)(2,1)S(1)}, bf16[32,2,16,128]{3,2,1,0:T(8,128)(2,1)S(1)}, u32[]{:S(2)}, u32[]{:S(2)}) collective-permute-start(bf16[32,2,16,128]{3,2,1,0:T(8,128)(2,1)S(1)} %bitcast.102), channel_id=1, source_target_pairs={{0,6},{2,0},{4,2},{6,4},{8,14},{10,8},{12,10},{14,12},{1,7},{3,1},... | collective-permute-start | bytes 786440 | tf_op jit(solution)/shard_map/ppermute | solution.py:483
  97.3 26.5 %collective-permute-start.10 = (bf16[32,2,16,128]{3,2,1,0:T(8,128)(2,1)S(1)}, bf16[32,2,16,128]{3,2,1,0:T(8,128)(2,1)S(1)}, u32[]{:S(2)}, u32[]{:S(2)}) collective-permute-start(bf16[32,2,16,128]{3,2,1,0:T(8,128)(2,1)S(1)} %bitcast.101), channel_id=1, source_target_pairs={{0,14},{2,8},{4,10},{6,12},{8,6},{10,0},{12,2},{14,4},{1,15},{3,9}... | collective-permute-start | bytes 786440 | tf_op jit(solution)/shard_map/ppermute | solution.py:483
  117.0 12.2 %collective-permute-start.6 = (bf16[32,2,16,128]{3,2,1,0:T(8,128)(2,1)S(1)}, bf16[32,2,16,128]{3,2,1,0:T(8,128)(2,1)S(1)}, u32[]{:S(2)}, u32[]{:S(2)}) collective-permute-start(bf16[32,2,16,128]{3,2,1,0:T(8,128)(2,1)S(1)} %bitcast.100), channel_id=1, source_target_pairs={{0,8},{2,10},{4,12},{6,14},{8,0},{10,2},{12,4},{14,6},{1,9},{3,11}... | collective-permute-start | bytes 786440 | tf_op jit(solution)/shard_map/ppermute | solution.py:483
  117.4 33.9 %collective-permute-start.12 = (bf16[32,2,16,128]{3,2,1,0:T(8,128)(2,1)S(1)}, bf16[32,2,16,128]{3,2,1,0:T(8,128)(2,1)S(1)}, u32[]{:S(2)}, u32[]{:S(2)}) collective-permute-start(bf16[32,2,16,128]{3,2,1,0:T(8,128)(2,1)S(1)} %bitcast.99), channel_id=1, source_target_pairs={{0,4},{2,6},{4,0},{6,2},{8,12},{10,14},{12,8},{14,10},{1,5},{3,7},... | collective-permute-start | bytes 786440 | tf_op jit(solution)/shard_map/ppermute | solution.py:483
  117.8 33.6 %collective-permute-start.13 = (bf16[32,2,16,128]{3,2,1,0:T(8,128)(2,1)S(1)}, bf16[32,2,16,128]{3,2,1,0:T(8,128)(2,1)S(1)}, u32[]{:S(2)}, u32[]{:S(2)}) collective-permute-start(bf16[32,2,16,128]{3,2,1,0:T(8,128)(2,1)S(1)} %bitcast.98), channel_id=1, source_target_pairs={{0,12},{2,14},{4,8},{6,10},{8,4},{10,6},{12,0},{14,2},{1,13},{3,15... | collective-permute-start | bytes 786440 | tf_op jit(solution)/shard_map/ppermute | solution.py:483
  123.9 27.3 %collective-permute-start.11 = (bf16[96,2,16,128]{3,2,1,0:T(8,128)(2,1)S(1)}, bf16[96,2,16,128]{3,2,1,0:T(8,128)(2,1)S(1)}, u32[]{:S(2)}, u32[]{:S(2)}) collective-permute-start(bf16[96,2,16,128]{3,2,1,0:T(8,128)(2,1)S(1)} %bitcast.96), channel_id=1, source_target_pairs={{0,8},{2,10},{4,12},{6,14},{8,0},{10,2},{12,4},{14,6},{1,9},{3,11}... | collective-permute-start | bytes 2359304 | tf_op jit(solution)/shard_map/ppermute | solution.py:483
  151.5 28.8 %collective-permute-start.16 = (bf16[8,32,2,16,128]{4,3,2,1,0:T(8,128)(2,1)S(1)}, bf16[8,32,2,16,128]{4,3,2,1,0:T(8,128)(2,1)S(1)}, u32[]{:S(2)}, u32[]{:S(2)}) collective-permute-start(bf16[8,32,2,16,128]{4,3,2,1,0:T(8,128)(2,1)S(1)} %bitcast_dynamic-update-slice_fusion.refs_4_), channel_id=1, source_target_pairs={{0,1},{1,0},{2,3},{3,2},{4,5},{5,4},{6,7},{7,6},{8,9},{9,8},{10,11... | collective-permute-start | bytes 6291464 | tf_op jit(solution)/shard_map/ppermute | solution.py:483
  152.0 9.3 %collective-permute-start.15 = (bf16[2,20,2,16,128]{4,3,2,1,0:T(8,128)(2,1)S(1)}, bf16[2,20,2,16,128]{4,3,2,1,0:T(8,128)(2,1)S(1)}, u32[]{:S(2)}, u32[]{:S(2)}) collective-permute-start(bf16[2,20,2,16,128]{4,3,2,1,0:T(8,128)(2,1)S(1)} %pad_maximum_fusion.3), channel_id=1, source_target_pairs={{0,2},{2,4},{4,6},{6,0},{8,10},{10,12},{12,14},{14,8},{1,3},{3,5},... | collective-permute-start | bytes 983048 | tf_op jit(solution)/shard_map/ppermute | solution.py:483
  152.1 28.2 %collective-permute-start.14 = (bf16[2,20,2,16,128]{4,3,2,1,0:T(8,128)(2,1)S(1)}, bf16[2,20,2,16,128]{4,3,2,1,0:T(8,128)(2,1)S(1)}, u32[]{:S(2)}, u32[]{:S(2)}) collective-permute-start(bf16[2,20,2,16,128]{4,3,2,1,0:T(8,128)(2,1)S(1)} %pad_maximum_fusion.2), channel_id=1, source_target_pairs={{0,4},{2,6},{4,0},{6,2},{8,12},{10,14},{12,8},{14,10},{1,5},{3,7},... | collective-permute-start | bytes 983048 | tf_op jit(solution)/shard_map/ppermute | solution.py:483
  154.1 29.2 %collective-permute-start.21 = (bf16[2,20,2,16,128]{4,3,2,1,0:T(8,128)(2,1)S(1)}, bf16[2,20,2,16,128]{4,3,2,1,0:T(8,128)(2,1)S(1)}, u32[]{:S(2)}, u32[]{:S(2)}) collective-permute-start(bf16[2,20,2,16,128]{4,3,2,1,0:T(8,128)(2,1)S(1)} %pad_maximum_fusion.4), channel_id=1, source_target_pairs={{0,6},{2,0},{4,2},{6,4},{8,14},{10,8},{12,10},{14,12},{1,7},{3,1},... | collective-permute-start | bytes 983048 | tf_op jit(solution)/shard_map/ppermute | solution.py:483
  161.3 6.5 %collective-permute-start.17 = (bf16[32,2,16,128]{3,2,1,0:T(8,128)(2,1)S(1)}, bf16[32,2,16,128]{3,2,1,0:T(8,128)(2,1)S(1)}, u32[]{:S(2)}, u32[]{:S(2)}) collective-permute-start(bf16[32,2,16,128]{3,2,1,0:T(8,128)(2,1)S(1)} %bitcast.97), channel_id=1, source_target_pairs={{0,8},{2,10},{4,12},{6,14},{8,0},{10,2},{12,4},{14,6},{1,9},{3,11}... | collective-permute-start | bytes 786440 | tf_op jit(solution)/shard_map/ppermute | solution.py:483
  183.5 3.2 %collective-permute-start.22 = (bf16[8,20,2,16,128]{4,3,2,1,0:T(8,128)(2,1)S(1)}, bf16[8,20,2,16,128]{4,3,2,1,0:T(8,128)(2,1)S(1)}, u32[]{:S(2)}, u32[]{:S(2)}) collective-permute-start(bf16[8,20,2,16,128]{4,3,2,1,0:T(8,128)(2,1)S(1)} %bitcast.86), channel_id=1, source_target_pairs={{0,1},{1,0},{2,3},{3,2},{4,5},{5,4},{6,7},{7,6},{8,9},{9,8},{10,11... | collective-permute-start | bytes 3932168 | tf_op jit(solution)/shard_map/ppermute | solution.py:483
  184.1 17.2 %collective-permute-start.18 = (bf16[2,12,2,16,128]{4,3,2,1,0:T(8,128)(2,1)S(1)}, bf16[2,12,2,16,128]{4,3,2,1,0:T(8,128)(2,1)S(1)}, u32[]{:S(2)}, u32[]{:S(2)}) collective-permute-start(bf16[2,12,2,16,128]{4,3,2,1,0:T(8,128)(2,1)S(1)} %pad_maximum_fusion.5), channel_id=1, source_target_pairs={{0,2},{2,4},{4,6},{6,0},{8,10},{10,12},{12,14},{14,8},{1,3},{3,5},... | collective-permute-start | bytes 589832 | tf_op jit(solution)/shard_map/ppermute | solution.py:483
  184.1 17.2 %collective-permute-start.19 = (bf16[2,12,2,16,128]{4,3,2,1,0:T(8,128)(2,1)S(1)}, bf16[2,12,2,16,128]{4,3,2,1,0:T(8,128)(2,1)S(1)}, u32[]{:S(2)}, u32[]{:S(2)}) collective-permute-start(bf16[2,12,2,16,128]{4,3,2,1,0:T(8,128)(2,1)S(1)} %pad_maximum_fusion.6), channel_id=1, source_target_pairs={{0,4},{2,6},{4,0},{6,2},{8,12},{10,14},{12,8},{14,10},{1,5},{3,7},... | collective-permute-start | bytes 589832 | tf_op jit(solution)/shard_map/ppermute | solution.py:483
  184.5 18.0 %collective-permute-start.20 = (bf16[2,12,2,16,128]{4,3,2,1,0:T(8,128)(2,1)S(1)}, bf16[2,12,2,16,128]{4,3,2,1,0:T(8,128)(2,1)S(1)}, u32[]{:S(2)}, u32[]{:S(2)}) collective-permute-start(bf16[2,12,2,16,128]{4,3,2,1,0:T(8,128)(2,1)S(1)} %pad_maximum_fusion.7), channel_id=1, source_target_pairs={{0,6},{2,0},{4,2},{6,4},{8,14},{10,8},{12,10},{14,12},{1,7},{3,1},... | collective-permute-start | bytes 589832 | tf_op jit(solution)/shard_map/ppermute | solution.py:483
  202.6 2.4 %collective-permute-start.23 = (bf16[8,12,2,16,128]{4,3,2,1,0:T(8,128)(2,1)S(1)}, bf16[8,12,2,16,128]{4,3,2,1,0:T(8,128)(2,1)S(1)}, u32[]{:S(2)}, u32[]{:S(2)}) collective-permute-start(bf16[8,12,2,16,128]{4,3,2,1,0:T(8,128)(2,1)S(1)} %bitcast.88), channel_id=1, source_target_pairs={{0,1},{1,0},{2,3},{3,2},{4,5},{5,4},{6,7},{7,6},{8,9},{9,8},{10,11... | collective-permute-start | bytes 2359304 | tf_op jit(solution)/shard_map/ppermute | solution.py:483
  (8 other events, 200.0 us)

commit v3 on v1

--- a/solution.py
+++ b/solution.py
@@ -500,7 +500,7 @@
     def columns(near, far):
         return jnp.stack([near, far])
 
-    cut = bands * 9 // 16
+    cut = bands * 5 // 8
     rest = bands - cut
     pairs = [(x, z) for z in range(time_count) for x in range(chan_count)]
     early_pairs = [(x, z) for z in (1, 3) for x in range(2)]
@@ -540,9 +540,11 @@
 
     blocks = {z: mix(0, z, -cut, far, cut) for z in hops}
     order = [2, 1, 3]
-    values, held = after([blocks[z] for z in order], [early[p] for p in late_pairs[:1]])
-    early.update(zip(late_pairs[:1], held))
-    two, one, three = (over(value, 0, z) for value, z in zip(values, order))
+    sent = []
+    for z in order:
+        (value,), (early[0, 2],) = after([blocks[z]], [early[0, 2]])
+        sent.append(over(value, 0, z))
+    two, one, three = sent
     (home,), (one,) = after([home], [one])
     home = over(home, 1, 0)
     low = [mix(0, 0, 0, home, cut), one, two, three]

time: 217 us -> 217 us (level)
  starting transfers between devices: 29.6 us -> 34.1 us
  waiting for transfers between devices: 122 us -> 118 us
    ppermute x24, starting transfers between devices: 29.6 us -> 34.1 us  [travel(): return lax.ppermute(value, axes, pairs)]
    ppermute x24, waiting for transfers between devices: 122 us -> 118 us  [travel(): return lax.ppermute(value, axes, pairs)]
  transfers between devices with their start and end apart: 24 -> 24, of which waited for: 15 -> 12; matrix products, arithmetic and copies ran while one was open for 2% -> 2% of each run, Pallas kernels for 21% -> 21%
where the time goes in v3:
time: 217 us; the launch traced here: 216 us
  waiting for transfers between devices  118 us (54%)
  Pallas kernels  55.3 us (25%)
  starting transfers between devices  34.1 us (16%)
  local copies, waits for them, and re-layouts  7.09 us (3%)
    ppermute x24, waiting for transfers between devices, travel(): return lax.ppermute(value, axes, pairs)  118 us
    ppermute x24, starting transfers between devices, travel(): return lax.ppermute(value, axes, pairs)  34.1 us
    pallas_call x2, Pallas kernels, channelise(): pl.pallas_call(lambda *refs: channelise_kernel(frames, chunk, columns, pl...  31.1 us
    pallas_call x2, Pallas kernels, correlate_tiles(): pl.pallas_call(lambda *refs: correlate_kernel(starts, width, *refs), grid...  24.2 us
  transfers between devices with their start and end apart: 24, of which 12 were waited for; matrix products, arithmetic and copies ran while one was open for 2% of the time, Pallas kernels for 21%

profile of v3, /device:TPU:11, one launch (start us, length us, event | category | flops | bytes accessed | tf_op | source)
XLA Modules:
  0.0 216.3 jit_solution(15454842970268494909)
XLA Ops:
  2.5 3.0 %constant_dynamic-slice_fusion = (bf16[2,16,8192]{2,1,0:T(8,128)(2,1)}, bf16[2,16,8192]{2,1,0:T(8,128)(2,1)S(1)}, bf16[2,16,8192]{2,1,0:T(8,128)(2,1)S(1)}, bf16[2,16,8192]{2,1,0:T(8,128)(2,1)}, bf16[2,16,8192]{2,1,0:T(8,128)(2,1)}) fusion(bf16[2,128,8192]{2,1,0:T(8,128)(2,1)} %bitcast.90, s32[]{:T(128)S(6)} %select_n.109, s32[]{:T(128)S(6)} %select_n.108, ...), kind=kLoop, calls=%fused_computation.137 | loop fusion | bytes 5242900 | tf_op jit(solution)/shard_map/dynamic_slice | solution.py:490
  7.3 6.6 %collective-permute-done.refs_2_ = bf16[2,16,8192]{2,1,0:T(8,128)(2,1)S(1)} collective-permute-done((bf16[2,16,8192]{2,1,0:T(8,128)(2,1)S(1)}, bf16[2,16,8192]{2,1,0:T(8,128)(2,1)S(1)}, u32[]{:S(2)}, u32[]{:S(2)}) %collective-permute-start) | collective-permute-done | bytes 524320 | tf_op jit(solution)/shard_map/ppermute | solution.py:483
  13.9 2.1 collective-permute-start.2
  16.1 30.7 %collective-permute-done.1.refs_3_ = bf16[2,16,8192]{2,1,0:T(8,128)(2,1)S(1)} collective-permute-done((bf16[2,16,8192]{2,1,0:T(8,128)(2,1)S(1)}, bf16[2,16,8192]{2,1,0:T(8,128)(2,1)S(1)}, u32[]{:S(2)}, u32[]{:S(2)}) %collective-permute-start.1) | collective-permute-done | bytes 524320 | tf_op jit(solution)/shard_map/ppermute | solution.py:483
  48.8 9.7 %collective-permute-done.3.refs_2_ = bf16[2,16,8192]{2,1,0:T(8,128)(2,1)S(1)} collective-permute-done((bf16[2,16,8192]{2,1,0:T(8,128)(2,1)}, bf16[2,16,8192]{2,1,0:T(8,128)(2,1)S(1)}, u32[]{:S(2)}, u32[]{:S(2)}) %collective-permute-start.3) | collective-permute-done | bytes 524320 | tf_op jit(solution)/shard_map/ppermute | solution.py:483
  58.4 4.1 %collective-permute-start.4 = (bf16[2,16,8192]{2,1,0:T(8,128)(2,1)}, bf16[2,16,8192]{2,1,0:T(8,128)(2,1)S(1)}, u32[]{:S(2)}, u32[]{:S(2)}) collective-permute-start(bf16[2,16,8192]{2,1,0:T(8,128)(2,1)} %get-tuple-element.73), channel_id=1, source_target_pairs={{0,4},{2,6},{4,0},{6,2},{8,12},{10,14},{12,8},{14,10},{1,5},{3,7},... | collective-permute-start | bytes 1572872 | tf_op jit(solution)/shard_map/ppermute | solution.py:483
  62.6 2.2 %copy-done = bf16[2,1,128,8192]{3,2,1,0:T(8,128)(2,1)S(1)} copy-done((bf16[2,1,128,8192]{3,2,1,0:T(8,128)(2,1)S(1)}, bf16[2,1,128,8192]{3,2,1,0:T(8,128)(2,1)}, u32[]{:S(2)}) %copy-start) | copy-done | bytes 4194328
  64.8 15.6 %channelise.2 = (bf16[1024,128]{1,0:T(8,128)(2,1)S(1)}, bf16[1024,128]{1,0:T(8,128)(2,1)S(1)}, bf16[1024,128]{1,0:T(8,128)(2,1)S(1)}, bf16[1024,128]{1,0:T(8,128...) custom-call(s32[3]{0:T(128)S(1)} %pad_add_fusion.refs_0_, ...), custom_call_target="tpu_custom_call" | custom-call | flops 8999999488 | bytes 4194304 | tf_op jit(solution)/shard_map/channelise/pallas_call | solution.py:276
  80.3 13.3 %collective-permute-done.4.refs_3_ = bf16[2,16,8192]{2,1,0:T(8,128)(2,1)S(1)} collective-permute-done((bf16[2,16,8192]{2,1,0:T(8,128)(2,1)}, bf16[2,16,8192]{2,1,0:T(8,128)(2,1)S(1)}, u32[]{:S(2)}, u32[]{:S(2)}) %collective-permute-start.4) | collective-permute-done | bytes 524320 | tf_op jit(solution)/shard_map/ppermute | solution.py:483
  93.6 1.9 collective-permute-start.7
  97.3 4.2 %collective-permute-start.10 = (bf16[32,2,16,128]{3,2,1,0:T(8,128)(2,1)S(1)}, bf16[32,2,16,128]{3,2,1,0:T(8,128)(2,1)S(1)}, u32[]{:S(2)}, u32[]{:S(2)}) collective-permute-start(bf16[32,2,16,128]{3,2,1,0:T(8,128)(2,1)S(1)} %bitcast.101), channel_id=1, source_target_pairs={{0,14},{2,8},{4,10},{6,12},{8,6},{10,0},{12,2},{14,4},{1,15},{3,9}... | collective-permute-start | bytes 786440 | tf_op jit(solution)/shard_map/ppermute | solution.py:483
  101.5 15.6 %channelise.3 = (bf16[4096,128]{1,0:T(8,128)(2,1)S(1)}, bf16[3072,128]{1,0:T(8,128)(2,1)S(1)}, bf16[1024,128]{1,0:T(8,128)(2,1)S(1)}) custom-call(s32[3]{0:T(128)S(1)} %pad_add_fusion.refs_0_, bf16[2,128,8192]{2,1,0:T(8,128)(2,1)S(1)} %bitcast.92, bf16[2,16,8192]{2,1,0:T(8,128)(2,1)S(1)} %collective-permute-done.3.refs_2_, ...), custom_call_target="tpu_custom_call" | custom-call | flops 8999999488 | bytes 4194304 | tf_op jit(solution)/shard_map/channelise/pallas_call | solution.py:276
  117.8 3.0 %collective-permute-start.13 = (bf16[32,2,16,128]{3,2,1,0:T(8,128)(2,1)S(1)}, bf16[32,2,16,128]{3,2,1,0:T(8,128)(2,1)S(1)}, u32[]{:S(2)}, u32[]{:S(2)}) collective-permute-start(bf16[32,2,16,128]{3,2,1,0:T(8,128)(2,1)S(1)} %bitcast.98), channel_id=1, source_target_pairs={{0,12},{2,14},{4,8},{6,10},{8,4},{10,6},{12,0},{14,2},{1,13},{3,15... | collective-permute-start | bytes 786440 | tf_op jit(solution)/shard_map/ppermute | solution.py:483
  120.8 3.1 %collective-permute-done.10 = bf16[32,2,16,128]{3,2,1,0:T(8,128)(2,1)S(1)} collective-permute-done((bf16[32,2,16,128]{3,2,1,0:T(8,128)(2,1)S(1)}, bf16[32,2,16,128]{3,2,1,0:T(8,128)(2,1)S(1)}, u32[]{:S(2)}, u32[]{:S(2)}) %collective-permute-start.10) | collective-permute-done | bytes 262176 | tf_op jit(solution)/shard_map/ppermute | solution.py:483
  125.1 4.2 %collective-permute-done.6 = bf16[32,2,16,128]{3,2,1,0:T(8,128)(2,1)S(1)} collective-permute-done((bf16[32,2,16,128]{3,2,1,0:T(8,128)(2,1)S(1)}, bf16[32,2,16,128]{3,2,1,0:T(8,128)(2,1)S(1)}, u32[]{:S(2)}, u32[]{:S(2)}) %collective-permute-start.6) | collective-permute-done | bytes 262176 | tf_op jit(solution)/shard_map/ppermute | solution.py:483
  129.4 21.7 %collective-permute-done.11 = bf16[96,2,16,128]{3,2,1,0:T(8,128)(2,1)S(1)} collective-permute-done((bf16[96,2,16,128]{3,2,1,0:T(8,128)(2,1)S(1)}, bf16[96,2,16,128]{3,2,1,0:T(8,128)(2,1)S(1)}, u32[]{:S(2)}, u32[]{:S(2)}) %collective-permute-start.11) | collective-permute-done | bytes 786464 | tf_op jit(solution)/shard_map/ppermute | solution.py:483
  154.2 7.1 %collective-permute-done.15 = bf16[2,20,2,16,128]{4,3,2,1,0:T(8,128)(2,1)S(1)} collective-permute-done((bf16[2,20,2,16,128]{4,3,2,1,0:T(8,128)(2,1)S(1)}, bf16[2,20,2,16,128]{4,3,2,1,0:T(8,128)(2,1)S(1)}, u32[]{:S(2)}, u32[]{:S(2)}) %collective-permute-start.15) | collective-permute-done | bytes 327712 | tf_op jit(solution)/shard_map/ppermute | solution.py:483
  162.6 5.3 %collective-permute-done.17 = bf16[32,2,16,128]{3,2,1,0:T(8,128)(2,1)S(1)} collective-permute-done((bf16[32,2,16,128]{3,2,1,0:T(8,128)(2,1)S(1)}, bf16[32,2,16,128]{3,2,1,0:T(8,128)(2,1)S(1)}, u32[]{:S(2)}, u32[]{:S(2)}) %collective-permute-start.17) | collective-permute-done | bytes 262176 | tf_op jit(solution)/shard_map/ppermute | solution.py:483
  167.9 12.4 %collective-permute-done.14 = bf16[2,20,2,16,128]{4,3,2,1,0:T(8,128)(2,1)S(1)} collective-permute-done((bf16[2,20,2,16,128]{4,3,2,1,0:T(8,128)(2,1)S(1)}, bf16[2,20,2,16,128]{4,3,2,1,0:T(8,128)(2,1)S(1)}, u32[]{:S(2)}, u32[]{:S(2)}) %collective-permute-start.14) | collective-permute-done | bytes 327712 | tf_op jit(solution)/shard_map/ppermute | solution.py:483
  182.9 4.0 %collective-permute-start.19 = (bf16[2,12,2,16,128]{4,3,2,1,0:T(8,128)(2,1)S(1)}, bf16[2,12,2,16,128]{4,3,2,1,0:T(8,128)(2,1)S(1)}, u32[]{:S(2)}, u32[]{:S(2)}) collective-permute-start(bf16[2,12,2,16,128]{4,3,2,1,0:T(8,128)(2,1)S(1)} %pad_maximum_fusion.6), channel_id=1, source_target_pairs={{0,4},{2,6},{4,0},{6,2},{8,12},{10,14},{12,8},{14,10},{1,5},{3,7},... | collective-permute-start | bytes 589832 | tf_op jit(solution)/shard_map/ppermute | solution.py:483
  186.9 14.5 %correlate.2.refs_8_ = f32[8,32,2,2,64,128]{5,4,3,2,1,0:T(8,128)} custom-call(s32[3]{0:T(128)S(1)} %pad_add_fusion.refs_0_, bf16[512,256]{1,0:T(8,128)(2,1)S(1)} %fusion.1.refs_1_, bf16[2,256,512]{2,1,0:T(8,128)(2,1)S(1)} %fusion.refs_2_, f32[8,256]{1,0:T(8,128)S(1)} %tile.10.refs_3_, ...), custom_call_target="tpu_custom_call" | custom-call | flops 8125000192 | bytes 27525120 | tf_op jit(solution)/shard_map/correlate/pallas_call | solution.py:401
  201.5 2.3 %collective-permute-done.20 = bf16[2,12,2,16,128]{4,3,2,1,0:T(8,128)(2,1)S(1)} collective-permute-done((bf16[2,12,2,16,128]{4,3,2,1,0:T(8,128)(2,1)S(1)}, bf16[2,12,2,16,128]{4,3,2,1,0:T(8,128)(2,1)S(1)}, u32[]{:S(2)}, u32[]{:S(2)}) %collective-permute-start.20) | collective-permute-done | bytes 196640 | tf_op jit(solution)/shard_map/ppermute | solution.py:483
  204.8 1.9 collective-permute-done.23.refs_7_
  206.7 9.6 %correlate.3 = f32[8,32,2,2,64,128]{5,4,3,2,1,0:T(8,128)} custom-call(s32[3]{0:T(128)S(1)} %pad_add_fusion.refs_0_, bf16[512,256]{1,0:T(8,128)(2,1)S(1)} %fusion.1.refs_1_, bf16[2,256,512]{2,1,0:T(8,128)(2,1)S(1)} %fusion.refs_2_, f32[8,256]{1,0:T(8,128)S(1)} %tile.10.refs_3_, ...), custom_call_target="tpu_custom_call", output_to_operand_aliasing={{}: (8, {})} | custom-call | flops 4874999808 | bytes 16515072 | tf_op jit(solution)/shard_map/correlate/pallas_call | solution.py:401
  (91 shorter events, 18.1 us)
Async XLA Ops:
  1.1 12.8 %collective-permute-start = (bf16[2,16,8192]{2,1,0:T(8,128)(2,1)S(1)}, bf16[2,16,8192]{2,1,0:T(8,128)(2,1)S(1)}, u32[]{:S(2)}, u32[]{:S(2)}) collective-permute-start(bf16[2,16,8192]{2,1,0:T(8,128)(2,1)S(1)} %dynamic-slice_bitcast_fusion), channel_id=1, source_target_pairs={{0,2},{2,4},{4,6},{6,0},{8,10},{10,12},{12,14},{14,8},{1,3},{3,5},... | collective-permute-start | bytes 1572872 | tf_op jit(solution)/shard_map/ppermute | solution.py:483
  5.5 41.3 %collective-permute-start.1 = (bf16[2,16,8192]{2,1,0:T(8,128)(2,1)S(1)}, bf16[2,16,8192]{2,1,0:T(8,128)(2,1)S(1)}, u32[]{:S(2)}, u32[]{:S(2)}) collective-permute-start(bf16[2,16,8192]{2,1,0:T(8,128)(2,1)S(1)} %get-tuple-element.121), channel_id=1, source_target_pairs={{0,4},{2,6},{4,0},{6,2},{8,12},{10,14},{12,8},{14,10},{1,5},{3,7},... | collective-permute-start | bytes 1572872 | tf_op jit(solution)/shard_map/ppermute | solution.py:483
  13.9 33.3 %collective-permute-start.2 = (bf16[2,16,8192]{2,1,0:T(8,128)(2,1)}, bf16[2,16,8192]{2,1,0:T(8,128)(2,1)S(1)}, u32[]{:S(2)}, u32[]{:S(2)}) collective-permute-start(bf16[2,16,8192]{2,1,0:T(8,128)(2,1)} %get-tuple-element.66), channel_id=1, source_target_pairs={{0,6},{2,0},{4,2},{6,4},{8,14},{10,8},{12,10},{14,12},{1,7},{3,1},... | collective-permute-start | bytes 1572872 | tf_op jit(solution)/shard_map/ppermute | solution.py:483
  46.7 11.7 %collective-permute-start.3 = (bf16[2,16,8192]{2,1,0:T(8,128)(2,1)}, bf16[2,16,8192]{2,1,0:T(8,128)(2,1)S(1)}, u32[]{:S(2)}, u32[]{:S(2)}) collective-permute-start(bf16[2,16,8192]{2,1,0:T(8,128)(2,1)} %get-tuple-element.72), channel_id=1, source_target_pairs={{0,2},{2,4},{4,6},{6,0},{8,10},{10,12},{12,14},{14,8},{1,3},{3,5},... | collective-permute-start | bytes 1572872 | tf_op jit(solution)/shard_map/ppermute | solution.py:483
  47.3 54.2 %collective-permute-start.5 = (bf16[2,16,8192]{2,1,0:T(8,128)(2,1)S(1)}, bf16[2,16,8192]{2,1,0:T(8,128)(2,1)S(1)}, u32[]{:S(2)}, u32[]{:S(2)}) collective-permute-start(bf16[2,16,8192]{2,1,0:T(8,128)(2,1)S(1)} %get-tuple-element.83), channel_id=1, source_target_pairs={{0,6},{2,0},{4,2},{6,4},{8,14},{10,8},{12,10},{14,12},{1,7},{3,1},... | collective-permute-start | bytes 1572872 | tf_op jit(solution)/shard_map/ppermute | solution.py:483
  58.4 35.2 %collective-permute-start.4 = (bf16[2,16,8192]{2,1,0:T(8,128)(2,1)}, bf16[2,16,8192]{2,1,0:T(8,128)(2,1)S(1)}, u32[]{:S(2)}, u32[]{:S(2)}) collective-permute-start(bf16[2,16,8192]{2,1,0:T(8,128)(2,1)} %get-tuple-element.73), channel_id=1, source_target_pairs={{0,4},{2,6},{4,0},{6,2},{8,12},{10,14},{12,8},{14,10},{1,5},{3,7},... | collective-permute-start | bytes 1572872 | tf_op jit(solution)/shard_map/ppermute | solution.py:483
  93.6 23.8 %collective-permute-start.7 = (bf16[32,2,16,128]{3,2,1,0:T(8,128)(2,1)S(1)}, bf16[32,2,16,128]{3,2,1,0:T(8,128)(2,1)S(1)}, u32[]{:S(2)}, u32[]{:S(2)}) collective-permute-start(bf16[32,2,16,128]{3,2,1,0:T(8,128)(2,1)S(1)} %bitcast.104), channel_id=1, source_target_pairs={{0,2},{2,4},{4,6},{6,0},{8,10},{10,12},{12,14},{14,8},{1,3},{3,5},... | collective-permute-start | bytes 786440 | tf_op jit(solution)/shard_map/ppermute | solution.py:483
  95.5 22.3 %collective-permute-start.8 = (bf16[32,2,16,128]{3,2,1,0:T(8,128)(2,1)S(1)}, bf16[32,2,16,128]{3,2,1,0:T(8,128)(2,1)S(1)}, u32[]{:S(2)}, u32[]{:S(2)}) collective-permute-start(bf16[32,2,16,128]{3,2,1,0:T(8,128)(2,1)S(1)} %bitcast.103), channel_id=1, source_target_pairs={{0,10},{2,12},{4,14},{6,8},{8,2},{10,4},{12,6},{14,0},{1,11},{3,13... | collective-permute-start | bytes 786440 | tf_op jit(solution)/shard_map/ppermute | solution.py:483
  96.9 23.9 %collective-permute-start.9 = (bf16[32,2,16,128]{3,2,1,0:T(8,128)(2,1)S(1)}, bf16[32,2,16,128]{3,2,1,0:T(8,128)(2,1)S(1)}, u32[]{:S(2)}, u32[]{:S(2)}) collective-permute-start(bf16[32,2,16,128]{3,2,1,0:T(8,128)(2,1)S(1)} %bitcast.102), channel_id=1, source_target_pairs={{0,6},{2,0},{4,2},{6,4},{8,14},{10,8},{12,10},{14,12},{1,7},{3,1},... | collective-permute-start | bytes 786440 | tf_op jit(solution)/shard_map/ppermute | solution.py:483
  97.3 26.5 %collective-permute-start.10 = (bf16[32,2,16,128]{3,2,1,0:T(8,128)(2,1)S(1)}, bf16[32,2,16,128]{3,2,1,0:T(8,128)(2,1)S(1)}, u32[]{:S(2)}, u32[]{:S(2)}) collective-permute-start(bf16[32,2,16,128]{3,2,1,0:T(8,128)(2,1)S(1)} %bitcast.101), channel_id=1, source_target_pairs={{0,14},{2,8},{4,10},{6,12},{8,6},{10,0},{12,2},{14,4},{1,15},{3,9}... | collective-permute-start | bytes 786440 | tf_op jit(solution)/shard_map/ppermute | solution.py:483
  117.0 12.2 %collective-permute-start.6 = (bf16[32,2,16,128]{3,2,1,0:T(8,128)(2,1)S(1)}, bf16[32,2,16,128]{3,2,1,0:T(8,128)(2,1)S(1)}, u32[]{:S(2)}, u32[]{:S(2)}) collective-permute-start(bf16[32,2,16,128]{3,2,1,0:T(8,128)(2,1)S(1)} %bitcast.100), channel_id=1, source_target_pairs={{0,8},{2,10},{4,12},{6,14},{8,0},{10,2},{12,4},{14,6},{1,9},{3,11}... | collective-permute-start | bytes 786440 | tf_op jit(solution)/shard_map/ppermute | solution.py:483
  117.4 33.9 %collective-permute-start.12 = (bf16[32,2,16,128]{3,2,1,0:T(8,128)(2,1)S(1)}, bf16[32,2,16,128]{3,2,1,0:T(8,128)(2,1)S(1)}, u32[]{:S(2)}, u32[]{:S(2)}) collective-permute-start(bf16[32,2,16,128]{3,2,1,0:T(8,128)(2,1)S(1)} %bitcast.99), channel_id=1, source_target_pairs={{0,4},{2,6},{4,0},{6,2},{8,12},{10,14},{12,8},{14,10},{1,5},{3,7},... | collective-permute-start | bytes 786440 | tf_op jit(solution)/shard_map/ppermute | solution.py:483
  117.8 33.6 %collective-permute-start.13 = (bf16[32,2,16,128]{3,2,1,0:T(8,128)(2,1)S(1)}, bf16[32,2,16,128]{3,2,1,0:T(8,128)(2,1)S(1)}, u32[]{:S(2)}, u32[]{:S(2)}) collective-permute-start(bf16[32,2,16,128]{3,2,1,0:T(8,128)(2,1)S(1)} %bitcast.98), channel_id=1, source_target_pairs={{0,12},{2,14},{4,8},{6,10},{8,4},{10,6},{12,0},{14,2},{1,13},{3,15... | collective-permute-start | bytes 786440 | tf_op jit(solution)/shard_map/ppermute | solution.py:483
  123.9 27.3 %collective-permute-start.11 = (bf16[96,2,16,128]{3,2,1,0:T(8,128)(2,1)S(1)}, bf16[96,2,16,128]{3,2,1,0:T(8,128)(2,1)S(1)}, u32[]{:S(2)}, u32[]{:S(2)}) collective-permute-start(bf16[96,2,16,128]{3,2,1,0:T(8,128)(2,1)S(1)} %bitcast.96), channel_id=1, source_target_pairs={{0,8},{2,10},{4,12},{6,14},{8,0},{10,2},{12,4},{14,6},{1,9},{3,11}... | collective-permute-start | bytes 2359304 | tf_op jit(solution)/shard_map/ppermute | solution.py:483
  151.5 28.8 %collective-permute-start.16 = (bf16[8,32,2,16,128]{4,3,2,1,0:T(8,128)(2,1)S(1)}, bf16[8,32,2,16,128]{4,3,2,1,0:T(8,128)(2,1)S(1)}, u32[]{:S(2)}, u32[]{:S(2)}) collective-permute-start(bf16[8,32,2,16,128]{4,3,2,1,0:T(8,128)(2,1)S(1)} %bitcast_dynamic-update-slice_fusion.refs_4_), channel_id=1, source_target_pairs={{0,1},{1,0},{2,3},{3,2},{4,5},{5,4},{6,7},{7,6},{8,9},{9,8},{10,11... | collective-permute-start | bytes 6291464 | tf_op jit(solution)/shard_map/ppermute | solution.py:483
  152.0 9.3 %collective-permute-start.15 = (bf16[2,20,2,16,128]{4,3,2,1,0:T(8,128)(2,1)S(1)}, bf16[2,20,2,16,128]{4,3,2,1,0:T(8,128)(2,1)S(1)}, u32[]{:S(2)}, u32[]{:S(2)}) collective-permute-start(bf16[2,20,2,16,128]{4,3,2,1,0:T(8,128)(2,1)S(1)} %pad_maximum_fusion.3), channel_id=1, source_target_pairs={{0,2},{2,4},{4,6},{6,0},{8,10},{10,12},{12,14},{14,8},{1,3},{3,5},... | collective-permute-start | bytes 983048 | tf_op jit(solution)/shard_map/ppermute | solution.py:483
  152.1 28.2 %collective-permute-start.21 = (bf16[2,20,2,16,128]{4,3,2,1,0:T(8,128)(2,1)S(1)}, bf16[2,20,2,16,128]{4,3,2,1,0:T(8,128)(2,1)S(1)}, u32[]{:S(2)}, u32[]{:S(2)}) collective-permute-start(bf16[2,20,2,16,128]{4,3,2,1,0:T(8,128)(2,1)S(1)} %pad_maximum_fusion.2), channel_id=1, source_target_pairs={{0,6},{2,0},{4,2},{6,4},{8,14},{10,8},{12,10},{14,12},{1,7},{3,1},... | collective-permute-start | bytes 983048 | tf_op jit(solution)/shard_map/ppermute | solution.py:483
  153.6 26.7 %collective-permute-start.14 = (bf16[2,20,2,16,128]{4,3,2,1,0:T(8,128)(2,1)S(1)}, bf16[2,20,2,16,128]{4,3,2,1,0:T(8,128)(2,1)S(1)}, u32[]{:S(2)}, u32[]{:S(2)}) collective-permute-start(bf16[2,20,2,16,128]{4,3,2,1,0:T(8,128)(2,1)S(1)} %pad_maximum_fusion.4), channel_id=1, source_target_pairs={{0,4},{2,6},{4,0},{6,2},{8,12},{10,14},{12,8},{14,10},{1,5},{3,7},... | collective-permute-start | bytes 983048 | tf_op jit(solution)/shard_map/ppermute | solution.py:483
  161.3 6.5 %collective-permute-start.17 = (bf16[32,2,16,128]{3,2,1,0:T(8,128)(2,1)S(1)}, bf16[32,2,16,128]{3,2,1,0:T(8,128)(2,1)S(1)}, u32[]{:S(2)}, u32[]{:S(2)}) collective-permute-start(bf16[32,2,16,128]{3,2,1,0:T(8,128)(2,1)S(1)} %bitcast.97), channel_id=1, source_target_pairs={{0,8},{2,10},{4,12},{6,14},{8,0},{10,2},{12,4},{14,6},{1,9},{3,11}... | collective-permute-start | bytes 786440 | tf_op jit(solution)/shard_map/ppermute | solution.py:483
  180.4 6.5 %collective-permute-start.22 = (bf16[8,20,2,16,128]{4,3,2,1,0:T(8,128)(2,1)S(1)}, bf16[8,20,2,16,128]{4,3,2,1,0:T(8,128)(2,1)S(1)}, u32[]{:S(2)}, u32[]{:S(2)}) collective-permute-start(bf16[8,20,2,16,128]{4,3,2,1,0:T(8,128)(2,1)S(1)} %bitcast.86), channel_id=1, source_target_pairs={{0,1},{1,0},{2,3},{3,2},{4,5},{5,4},{6,7},{7,6},{8,9},{9,8},{10,11... | collective-permute-start | bytes 3932168 | tf_op jit(solution)/shard_map/ppermute | solution.py:483
  181.3 20.1 %collective-permute-start.18 = (bf16[2,12,2,16,128]{4,3,2,1,0:T(8,128)(2,1)S(1)}, bf16[2,12,2,16,128]{4,3,2,1,0:T(8,128)(2,1)S(1)}, u32[]{:S(2)}, u32[]{:S(2)}) collective-permute-start(bf16[2,12,2,16,128]{4,3,2,1,0:T(8,128)(2,1)S(1)} %pad_maximum_fusion.5), channel_id=1, source_target_pairs={{0,2},{2,4},{4,6},{6,0},{8,10},{10,12},{12,14},{14,8},{1,3},{3,5},... | collective-permute-start | bytes 589832 | tf_op jit(solution)/shard_map/ppermute | solution.py:483
  182.9 18.6 %collective-permute-start.19 = (bf16[2,12,2,16,128]{4,3,2,1,0:T(8,128)(2,1)S(1)}, bf16[2,12,2,16,128]{4,3,2,1,0:T(8,128)(2,1)S(1)}, u32[]{:S(2)}, u32[]{:S(2)}) collective-permute-start(bf16[2,12,2,16,128]{4,3,2,1,0:T(8,128)(2,1)S(1)} %pad_maximum_fusion.6), channel_id=1, source_target_pairs={{0,4},{2,6},{4,0},{6,2},{8,12},{10,14},{12,8},{14,10},{1,5},{3,7},... | collective-permute-start | bytes 589832 | tf_op jit(solution)/shard_map/ppermute | solution.py:483
  186.9 16.9 %collective-permute-start.20 = (bf16[2,12,2,16,128]{4,3,2,1,0:T(8,128)(2,1)S(1)}, bf16[2,12,2,16,128]{4,3,2,1,0:T(8,128)(2,1)S(1)}, u32[]{:S(2)}, u32[]{:S(2)}) collective-permute-start(bf16[2,12,2,16,128]{4,3,2,1,0:T(8,128)(2,1)S(1)} %pad_maximum_fusion.7), channel_id=1, source_target_pairs={{0,6},{2,0},{4,2},{6,4},{8,14},{10,8},{12,10},{14,12},{1,7},{3,1},... | collective-permute-start | bytes 589832 | tf_op jit(solution)/shard_map/ppermute | solution.py:483
  203.9 2.8 %collective-permute-start.23 = (bf16[8,12,2,16,128]{4,3,2,1,0:T(8,128)(2,1)S(1)}, bf16[8,12,2,16,128]{4,3,2,1,0:T(8,128)(2,1)S(1)}, u32[]{:S(2)}, u32[]{:S(2)}) collective-permute-start(bf16[8,12,2,16,128]{4,3,2,1,0:T(8,128)(2,1)S(1)} %bitcast.88), channel_id=1, source_target_pairs={{0,1},{1,0},{2,3},{3,2},{4,5},{5,4},{6,7},{7,6},{8,9},{9,8},{10,11... | collective-permute-start | bytes 2359304 | tf_op jit(solution)/shard_map/ppermute | solution.py:483
  (8 other events, 200.0 us)

commit v4 on v1

--- a/solution.py
+++ b/solution.py
@@ -252,7 +252,7 @@
                     part * LANES : (part + 1) * LANES, half * LANES : (half + 1) * LANES
                 ]
 
-    share = w_ref.shape[0] // (columns * sources)
+    share = length // AVG * 2 * ROWS // (columns * sources)
     band_rows = 2 * ROWS
     piece = 2 * band_rows
     for blocks, out_ref in zip(plan, out_refs):
@@ -285,9 +285,9 @@
         scratch_shapes=[
             pltpu.VMEM((sources, 2, ROWS, frames * length), jnp.bfloat16),
             pltpu.VMEM((RADIX, spectra, 2, ROWS, LANES), jnp.float32),
-            pltpu.VMEM((ROWS * RADIX * spectra, LANES), jnp.float32),
-            pltpu.VMEM((ROWS * RADIX * spectra, LANES), jnp.float32),
-            pltpu.VMEM((out_rows, LANES), jnp.float32),
+            pltpu.VMEM(((ROWS + 1) * RADIX * spectra, LANES), jnp.float32),
+            pltpu.VMEM(((ROWS + 1) * RADIX * spectra, LANES), jnp.float32),
+            pltpu.VMEM((out_rows + out_rows // LANES, LANES), jnp.float32),
             pltpu.SemaphoreType.DMA((sources,)),
         ],
         compiler_params=pltpu.CompilerParams(vmem_limit_bytes=40 * 2**20),
@@ -500,7 +500,7 @@
     def columns(near, far):
         return jnp.stack([near, far])
 
-    cut = bands * 9 // 16
+    cut = bands * 5 // 8
     rest = bands - cut
     pairs = [(x, z) for z in range(time_count) for x in range(chan_count)]
     early_pairs = [(x, z) for z in (1, 3) for x in range(2)]

time: 217 us -> 216 us (level)
  transfers between devices with their start and end apart: 24 -> 24, of which waited for: 15 -> 14; matrix products, arithmetic and copies ran while one was open for 2% -> 2% of each run, Pallas kernels for 21% -> 21%
where the time goes in v4:
time: 216 us; the launch traced here: 215 us
  waiting for transfers between devices  121 us (56%)
  Pallas kernels  55.2 us (26%)
  starting transfers between devices  29.6 us (14%)
  local copies, waits for them, and re-layouts  7.09 us (3%)
    ppermute x24, waiting for transfers between devices, travel(): return lax.ppermute(value, axes, pairs)  121 us
    pallas_call x2, Pallas kernels, channelise(): pl.pallas_call(lambda *refs: channelise_kernel(frames, chunk, columns, pl...  31.1 us
    ppermute x24, starting transfers between devices, travel(): return lax.ppermute(value, axes, pairs)  29.6 us
    pallas_call x2, Pallas kernels, correlate_tiles(): pl.pallas_call(lambda *refs: correlate_kernel(starts, width, *refs), grid...  24.1 us
  transfers between devices with their start and end apart: 24, of which 14 were waited for; matrix products, arithmetic and copies ran while one was open for 2% of the time, Pallas kernels for 21%

profile of v4, /device:TPU:11, one launch (start us, length us, event | category | flops | bytes accessed | tf_op | source)
XLA Modules:
  0.0 214.7 jit_solution(7691027681202111702)
XLA Ops:
  2.5 3.0 %constant_dynamic-slice_fusion = (bf16[2,16,8192]{2,1,0:T(8,128)(2,1)}, bf16[2,16,8192]{2,1,0:T(8,128)(2,1)S(1)}, bf16[2,16,8192]{2,1,0:T(8,128)(2,1)S(1)}, bf16[2,16,8192]{2,1,0:T(8,128)(2,1)}, bf16[2,16,8192]{2,1,0:T(8,128)(2,1)}) fusion(bf16[2,128,8192]{2,1,0:T(8,128)(2,1)} %bitcast.90, s32[]{:T(128)S(6)} %select_n.109, s32[]{:T(128)S(6)} %select_n.108, ...), kind=kLoop, calls=%fused_computation.137 | loop fusion | bytes 5242900 | tf_op jit(solution)/shard_map/dynamic_slice | solution.py:490
  7.3 6.6 %collective-permute-done.refs_2_ = bf16[2,16,8192]{2,1,0:T(8,128)(2,1)S(1)} collective-permute-done((bf16[2,16,8192]{2,1,0:T(8,128)(2,1)S(1)}, bf16[2,16,8192]{2,1,0:T(8,128)(2,1)S(1)}, u32[]{:S(2)}, u32[]{:S(2)}) %collective-permute-start) | collective-permute-done | bytes 524320 | tf_op jit(solution)/shard_map/ppermute | solution.py:483
  13.9 2.1 collective-permute-start.2
  16.1 30.7 %collective-permute-done.1.refs_3_ = bf16[2,16,8192]{2,1,0:T(8,128)(2,1)S(1)} collective-permute-done((bf16[2,16,8192]{2,1,0:T(8,128)(2,1)S(1)}, bf16[2,16,8192]{2,1,0:T(8,128)(2,1)S(1)}, u32[]{:S(2)}, u32[]{:S(2)}) %collective-permute-start.1) | collective-permute-done | bytes 524320 | tf_op jit(solution)/shard_map/ppermute | solution.py:483
  48.8 9.7 %collective-permute-done.3.refs_2_ = bf16[2,16,8192]{2,1,0:T(8,128)(2,1)S(1)} collective-permute-done((bf16[2,16,8192]{2,1,0:T(8,128)(2,1)}, bf16[2,16,8192]{2,1,0:T(8,128)(2,1)S(1)}, u32[]{:S(2)}, u32[]{:S(2)}) %collective-permute-start.3) | collective-permute-done | bytes 524320 | tf_op jit(solution)/shard_map/ppermute | solution.py:483
  58.4 4.1 %collective-permute-start.4 = (bf16[2,16,8192]{2,1,0:T(8,128)(2,1)}, bf16[2,16,8192]{2,1,0:T(8,128)(2,1)S(1)}, u32[]{:S(2)}, u32[]{:S(2)}) collective-permute-start(bf16[2,16,8192]{2,1,0:T(8,128)(2,1)} %get-tuple-element.71), channel_id=1, source_target_pairs={{0,4},{2,6},{4,0},{6,2},{8,12},{10,14},{12,8},{14,10},{1,5},{3,7},... | collective-permute-start | bytes 1572872 | tf_op jit(solution)/shard_map/ppermute | solution.py:483
  62.6 2.2 %copy-done = bf16[2,1,128,8192]{3,2,1,0:T(8,128)(2,1)S(1)} copy-done((bf16[2,1,128,8192]{3,2,1,0:T(8,128)(2,1)S(1)}, bf16[2,1,128,8192]{3,2,1,0:T(8,128)(2,1)}, u32[]{:S(2)}) %copy-start) | copy-done | bytes 4194328
  64.8 15.6 %channelise.2 = (bf16[1024,128]{1,0:T(8,128)(2,1)S(1)}, bf16[1024,128]{1,0:T(8,128)(2,1)S(1)}, bf16[1024,128]{1,0:T(8,128)(2,1)S(1)}, bf16[1024,128]{1,0:T(8,128...) custom-call(s32[3]{0:T(128)S(1)} %pad_add_fusion.refs_0_, ...), custom_call_target="tpu_custom_call" | custom-call | flops 8999999488 | bytes 4194304 | tf_op jit(solution)/shard_map/channelise/pallas_call | solution.py:276
  80.3 13.3 %collective-permute-done.4.refs_3_ = bf16[2,16,8192]{2,1,0:T(8,128)(2,1)S(1)} collective-permute-done((bf16[2,16,8192]{2,1,0:T(8,128)(2,1)}, bf16[2,16,8192]{2,1,0:T(8,128)(2,1)S(1)}, u32[]{:S(2)}, u32[]{:S(2)}) %collective-permute-start.4) | collective-permute-done | bytes 524320 | tf_op jit(solution)/shard_map/ppermute | solution.py:483
  93.6 1.9 collective-permute-start.7
  97.3 4.2 %collective-permute-start.10 = (bf16[32,2,16,128]{3,2,1,0:T(8,128)(2,1)S(1)}, bf16[32,2,16,128]{3,2,1,0:T(8,128)(2,1)S(1)}, u32[]{:S(2)}, u32[]{:S(2)}) collective-permute-start(bf16[32,2,16,128]{3,2,1,0:T(8,128)(2,1)S(1)} %bitcast.101), channel_id=1, source_target_pairs={{0,14},{2,8},{4,10},{6,12},{8,6},{10,0},{12,2},{14,4},{1,15},{3,9}... | collective-permute-start | bytes 786440 | tf_op jit(solution)/shard_map/ppermute | solution.py:483
  101.5 15.6 %channelise.3 = (bf16[4096,128]{1,0:T(8,128)(2,1)S(1)}, bf16[3072,128]{1,0:T(8,128)(2,1)S(1)}, bf16[1024,128]{1,0:T(8,128)(2,1)S(1)}) custom-call(s32[3]{0:T(128)S(1)} %pad_add_fusion.refs_0_, bf16[2,128,8192]{2,1,0:T(8,128)(2,1)S(1)} %bitcast.92, bf16[2,16,8192]{2,1,0:T(8,128)(2,1)S(1)} %collective-permute-done.3.refs_2_, ...), custom_call_target="tpu_custom_call" | custom-call | flops 8999999488 | bytes 4194304 | tf_op jit(solution)/shard_map/channelise/pallas_call | solution.py:276
  117.8 3.0 %collective-permute-start.13 = (bf16[32,2,16,128]{3,2,1,0:T(8,128)(2,1)S(1)}, bf16[32,2,16,128]{3,2,1,0:T(8,128)(2,1)S(1)}, u32[]{:S(2)}, u32[]{:S(2)}) collective-permute-start(bf16[32,2,16,128]{3,2,1,0:T(8,128)(2,1)S(1)} %bitcast.98), channel_id=1, source_target_pairs={{0,12},{2,14},{4,8},{6,10},{8,4},{10,6},{12,0},{14,2},{1,13},{3,15... | collective-permute-start | bytes 786440 | tf_op jit(solution)/shard_map/ppermute | solution.py:483
  120.8 3.1 %collective-permute-done.10 = bf16[32,2,16,128]{3,2,1,0:T(8,128)(2,1)S(1)} collective-permute-done((bf16[32,2,16,128]{3,2,1,0:T(8,128)(2,1)S(1)}, bf16[32,2,16,128]{3,2,1,0:T(8,128)(2,1)S(1)}, u32[]{:S(2)}, u32[]{:S(2)}) %collective-permute-start.10) | collective-permute-done | bytes 262176 | tf_op jit(solution)/shard_map/ppermute | solution.py:483
  125.1 4.2 %collective-permute-done.6 = bf16[32,2,16,128]{3,2,1,0:T(8,128)(2,1)S(1)} collective-permute-done((bf16[32,2,16,128]{3,2,1,0:T(8,128)(2,1)S(1)}, bf16[32,2,16,128]{3,2,1,0:T(8,128)(2,1)S(1)}, u32[]{:S(2)}, u32[]{:S(2)}) %collective-permute-start.6) | collective-permute-done | bytes 262176 | tf_op jit(solution)/shard_map/ppermute | solution.py:483
  129.4 21.7 %collective-permute-done.11 = bf16[96,2,16,128]{3,2,1,0:T(8,128)(2,1)S(1)} collective-permute-done((bf16[96,2,16,128]{3,2,1,0:T(8,128)(2,1)S(1)}, bf16[96,2,16,128]{3,2,1,0:T(8,128)(2,1)S(1)}, u32[]{:S(2)}, u32[]{:S(2)}) %collective-permute-start.11) | collective-permute-done | bytes 786464 | tf_op jit(solution)/shard_map/ppermute | solution.py:483
  152.1 2.1 collective-permute-start.14
  154.2 7.2 %collective-permute-done.15 = bf16[2,20,2,16,128]{4,3,2,1,0:T(8,128)(2,1)S(1)} collective-permute-done((bf16[2,20,2,16,128]{4,3,2,1,0:T(8,128)(2,1)S(1)}, bf16[2,20,2,16,128]{4,3,2,1,0:T(8,128)(2,1)S(1)}, u32[]{:S(2)}, u32[]{:S(2)}) %collective-permute-start.15) | collective-permute-done | bytes 327712 | tf_op jit(solution)/shard_map/ppermute | solution.py:483
  162.6 5.3 %collective-permute-done.17 = bf16[32,2,16,128]{3,2,1,0:T(8,128)(2,1)S(1)} collective-permute-done((bf16[32,2,16,128]{3,2,1,0:T(8,128)(2,1)S(1)}, bf16[32,2,16,128]{3,2,1,0:T(8,128)(2,1)S(1)}, u32[]{:S(2)}, u32[]{:S(2)}) %collective-permute-start.17) | collective-permute-done | bytes 262176 | tf_op jit(solution)/shard_map/ppermute | solution.py:483
  167.9 12.4 %collective-permute-done.14 = bf16[2,20,2,16,128]{4,3,2,1,0:T(8,128)(2,1)S(1)} collective-permute-done((bf16[2,20,2,16,128]{4,3,2,1,0:T(8,128)(2,1)S(1)}, bf16[2,20,2,16,128]{4,3,2,1,0:T(8,128)(2,1)S(1)}, u32[]{:S(2)}, u32[]{:S(2)}) %collective-permute-start.14) | collective-permute-done | bytes 327712 | tf_op jit(solution)/shard_map/ppermute | solution.py:483
  180.2 3.1 %collective-permute-done.21 = bf16[2,20,2,16,128]{4,3,2,1,0:T(8,128)(2,1)S(1)} collective-permute-done((bf16[2,20,2,16,128]{4,3,2,1,0:T(8,128)(2,1)S(1)}, bf16[2,20,2,16,128]{4,3,2,1,0:T(8,128)(2,1)S(1)}, u32[]{:S(2)}, u32[]{:S(2)}) %collective-permute-start.21) | collective-permute-done | bytes 327712 | tf_op jit(solution)/shard_map/ppermute | solution.py:483
  186.7 14.5 %correlate.2.refs_8_ = f32[8,32,2,2,64,128]{5,4,3,2,1,0:T(8,128)} custom-call(s32[3]{0:T(128)S(1)} %pad_add_fusion.refs_0_, bf16[512,256]{1,0:T(8,128)(2,1)S(1)} %fusion.1.refs_1_, bf16[2,256,512]{2,1,0:T(8,128)(2,1)S(1)} %fusion.refs_2_, f32[8,256]{1,0:T(8,128)S(1)} %tile.10.refs_3_, ...), custom_call_target="tpu_custom_call" | custom-call | flops 8125000192 | bytes 27525120 | tf_op jit(solution)/shard_map/correlate/pallas_call | solution.py:401
  203.2 1.9 collective-permute-done.23.refs_7_
  205.1 9.6 %correlate.3 = f32[8,32,2,2,64,128]{5,4,3,2,1,0:T(8,128)} custom-call(s32[3]{0:T(128)S(1)} %pad_add_fusion.refs_0_, bf16[512,256]{1,0:T(8,128)(2,1)S(1)} %fusion.1.refs_1_, bf16[2,256,512]{2,1,0:T(8,128)(2,1)S(1)} %fusion.refs_2_, f32[8,256]{1,0:T(8,128)S(1)} %tile.10.refs_3_, ...), custom_call_target="tpu_custom_call", output_to_operand_aliasing={{}: (8, {})} | custom-call | flops 4874999808 | bytes 16515072 | tf_op jit(solution)/shard_map/correlate/pallas_call | solution.py:401
  (91 shorter events, 17.6 us)
Async XLA Ops:
  1.1 12.8 %collective-permute-start = (bf16[2,16,8192]{2,1,0:T(8,128)(2,1)S(1)}, bf16[2,16,8192]{2,1,0:T(8,128)(2,1)S(1)}, u32[]{:S(2)}, u32[]{:S(2)}) collective-permute-start(bf16[2,16,8192]{2,1,0:T(8,128)(2,1)S(1)} %dynamic-slice_bitcast_fusion), channel_id=1, source_target_pairs={{0,2},{2,4},{4,6},{6,0},{8,10},{10,12},{12,14},{14,8},{1,3},{3,5},... | collective-permute-start | bytes 1572872 | tf_op jit(solution)/shard_map/ppermute | solution.py:483
  5.5 41.3 %collective-permute-start.1 = (bf16[2,16,8192]{2,1,0:T(8,128)(2,1)S(1)}, bf16[2,16,8192]{2,1,0:T(8,128)(2,1)S(1)}, u32[]{:S(2)}, u32[]{:S(2)}) collective-permute-start(bf16[2,16,8192]{2,1,0:T(8,128)(2,1)S(1)} %get-tuple-element.117), channel_id=1, source_target_pairs={{0,4},{2,6},{4,0},{6,2},{8,12},{10,14},{12,8},{14,10},{1,5},{3,7},... | collective-permute-start | bytes 1572872 | tf_op jit(solution)/shard_map/ppermute | solution.py:483
  13.9 33.3 %collective-permute-start.2 = (bf16[2,16,8192]{2,1,0:T(8,128)(2,1)}, bf16[2,16,8192]{2,1,0:T(8,128)(2,1)S(1)}, u32[]{:S(2)}, u32[]{:S(2)}) collective-permute-start(bf16[2,16,8192]{2,1,0:T(8,128)(2,1)} %get-tuple-element.64), channel_id=1, source_target_pairs={{0,6},{2,0},{4,2},{6,4},{8,14},{10,8},{12,10},{14,12},{1,7},{3,1},... | collective-permute-start | bytes 1572872 | tf_op jit(solution)/shard_map/ppermute | solution.py:483
  46.7 11.7 %collective-permute-start.3 = (bf16[2,16,8192]{2,1,0:T(8,128)(2,1)}, bf16[2,16,8192]{2,1,0:T(8,128)(2,1)S(1)}, u32[]{:S(2)}, u32[]{:S(2)}) collective-permute-start(bf16[2,16,8192]{2,1,0:T(8,128)(2,1)} %get-tuple-element.70), channel_id=1, source_target_pairs={{0,2},{2,4},{4,6},{6,0},{8,10},{10,12},{12,14},{14,8},{1,3},{3,5},... | collective-permute-start | bytes 1572872 | tf_op jit(solution)/shard_map/ppermute | solution.py:483
  47.3 54.2 %collective-permute-start.5 = (bf16[2,16,8192]{2,1,0:T(8,128)(2,1)S(1)}, bf16[2,16,8192]{2,1,0:T(8,128)(2,1)S(1)}, u32[]{:S(2)}, u32[]{:S(2)}) collective-permute-start(bf16[2,16,8192]{2,1,0:T(8,128)(2,1)S(1)} %get-tuple-element.81), channel_id=1, source_target_pairs={{0,6},{2,0},{4,2},{6,4},{8,14},{10,8},{12,10},{14,12},{1,7},{3,1},... | collective-permute-start | bytes 1572872 | tf_op jit(solution)/shard_map/ppermute | solution.py:483
  58.4 35.2 %collective-permute-start.4 = (bf16[2,16,8192]{2,1,0:T(8,128)(2,1)}, bf16[2,16,8192]{2,1,0:T(8,128)(2,1)S(1)}, u32[]{:S(2)}, u32[]{:S(2)}) collective-permute-start(bf16[2,16,8192]{2,1,0:T(8,128)(2,1)} %get-tuple-element.71), channel_id=1, source_target_pairs={{0,4},{2,6},{4,0},{6,2},{8,12},{10,14},{12,8},{14,10},{1,5},{3,7},... | collective-permute-start | bytes 1572872 | tf_op jit(solution)/shard_map/ppermute | solution.py:483
  93.6 23.8 %collective-permute-start.7 = (bf16[32,2,16,128]{3,2,1,0:T(8,128)(2,1)S(1)}, bf16[32,2,16,128]{3,2,1,0:T(8,128)(2,1)S(1)}, u32[]{:S(2)}, u32[]{:S(2)}) collective-permute-start(bf16[32,2,16,128]{3,2,1,0:T(8,128)(2,1)S(1)} %bitcast.104), channel_id=1, source_target_pairs={{0,2},{2,4},{4,6},{6,0},{8,10},{10,12},{12,14},{14,8},{1,3},{3,5},... | collective-permute-start | bytes 786440 | tf_op jit(solution)/shard_map/ppermute | solution.py:483
  95.5 22.3 %collective-permute-start.8 = (bf16[32,2,16,128]{3,2,1,0:T(8,128)(2,1)S(1)}, bf16[32,2,16,128]{3,2,1,0:T(8,128)(2,1)S(1)}, u32[]{:S(2)}, u32[]{:S(2)}) collective-permute-start(bf16[32,2,16,128]{3,2,1,0:T(8,128)(2,1)S(1)} %bitcast.103), channel_id=1, source_target_pairs={{0,10},{2,12},{4,14},{6,8},{8,2},{10,4},{12,6},{14,0},{1,11},{3,13... | collective-permute-start | bytes 786440 | tf_op jit(solution)/shard_map/ppermute | solution.py:483
  96.9 23.9 %collective-permute-start.9 = (bf16[32,2,16,128]{3,2,1,0:T(8,128)(2,1)S(1)}, bf16[32,2,16,128]{3,2,1,0:T(8,128)(2,1)S(1)}, u32[]{:S(2)}, u32[]{:S(2)}) collective-permute-start(bf16[32,2,16,128]{3,2,1,0:T(8,128)(2,1)S(1)} %bitcast.102), channel_id=1, source_target_pairs={{0,6},{2,0},{4,2},{6,4},{8,14},{10,8},{12,10},{14,12},{1,7},{3,1},... | collective-permute-start | bytes 786440 | tf_op jit(solution)/shard_map/ppermute | solution.py:483
  97.3 26.5 %collective-permute-start.10 = (bf16[32,2,16,128]{3,2,1,0:T(8,128)(2,1)S(1)}, bf16[32,2,16,128]{3,2,1,0:T(8,128)(2,1)S(1)}, u32[]{:S(2)}, u32[]{:S(2)}) collective-permute-start(bf16[32,2,16,128]{3,2,1,0:T(8,128)(2,1)S(1)} %bitcast.101), channel_id=1, source_target_pairs={{0,14},{2,8},{4,10},{6,12},{8,6},{10,0},{12,2},{14,4},{1,15},{3,9}... | collective-permute-start | bytes 786440 | tf_op jit(solution)/shard_map/ppermute | solution.py:483
  117.0 12.2 %collective-permute-start.6 = (bf16[32,2,16,128]{3,2,1,0:T(8,128)(2,1)S(1)}, bf16[32,2,16,128]{3,2,1,0:T(8,128)(2,1)S(1)}, u32[]{:S(2)}, u32[]{:S(2)}) collective-permute-start(bf16[32,2,16,128]{3,2,1,0:T(8,128)(2,1)S(1)} %bitcast.100), channel_id=1, source_target_pairs={{0,8},{2,10},{4,12},{6,14},{8,0},{10,2},{12,4},{14,6},{1,9},{3,11}... | collective-permute-start | bytes 786440 | tf_op jit(solution)/shard_map/ppermute | solution.py:483
  117.4 33.9 %collective-permute-start.12 = (bf16[32,2,16,128]{3,2,1,0:T(8,128)(2,1)S(1)}, bf16[32,2,16,128]{3,2,1,0:T(8,128)(2,1)S(1)}, u32[]{:S(2)}, u32[]{:S(2)}) collective-permute-start(bf16[32,2,16,128]{3,2,1,0:T(8,128)(2,1)S(1)} %bitcast.99), channel_id=1, source_target_pairs={{0,4},{2,6},{4,0},{6,2},{8,12},{10,14},{12,8},{14,10},{1,5},{3,7},... | collective-permute-start | bytes 786440 | tf_op jit(solution)/shard_map/ppermute | solution.py:483
  117.8 33.6 %collective-permute-start.13 = (bf16[32,2,16,128]{3,2,1,0:T(8,128)(2,1)S(1)}, bf16[32,2,16,128]{3,2,1,0:T(8,128)(2,1)S(1)}, u32[]{:S(2)}, u32[]{:S(2)}) collective-permute-start(bf16[32,2,16,128]{3,2,1,0:T(8,128)(2,1)S(1)} %bitcast.98), channel_id=1, source_target_pairs={{0,12},{2,14},{4,8},{6,10},{8,4},{10,6},{12,0},{14,2},{1,13},{3,15... | collective-permute-start | bytes 786440 | tf_op jit(solution)/shard_map/ppermute | solution.py:483
  123.9 27.3 %collective-permute-start.11 = (bf16[96,2,16,128]{3,2,1,0:T(8,128)(2,1)S(1)}, bf16[96,2,16,128]{3,2,1,0:T(8,128)(2,1)S(1)}, u32[]{:S(2)}, u32[]{:S(2)}) collective-permute-start(bf16[96,2,16,128]{3,2,1,0:T(8,128)(2,1)S(1)} %bitcast.96), channel_id=1, source_target_pairs={{0,8},{2,10},{4,12},{6,14},{8,0},{10,2},{12,4},{14,6},{1,9},{3,11}... | collective-permute-start | bytes 2359304 | tf_op jit(solution)/shard_map/ppermute | solution.py:483
  151.5 28.8 %collective-permute-start.16 = (bf16[8,32,2,16,128]{4,3,2,1,0:T(8,128)(2,1)S(1)}, bf16[8,32,2,16,128]{4,3,2,1,0:T(8,128)(2,1)S(1)}, u32[]{:S(2)}, u32[]{:S(2)}) collective-permute-start(bf16[8,32,2,16,128]{4,3,2,1,0:T(8,128)(2,1)S(1)} %bitcast_dynamic-update-slice_fusion.refs_4_), channel_id=1, source_target_pairs={{0,1},{1,0},{2,3},{3,2},{4,5},{5,4},{6,7},{7,6},{8,9},{9,8},{10,11... | collective-permute-start | bytes 6291464 | tf_op jit(solution)/shard_map/ppermute | solution.py:483
  152.0 9.3 %collective-permute-start.15 = (bf16[2,20,2,16,128]{4,3,2,1,0:T(8,128)(2,1)S(1)}, bf16[2,20,2,16,128]{4,3,2,1,0:T(8,128)(2,1)S(1)}, u32[]{:S(2)}, u32[]{:S(2)}) collective-permute-start(bf16[2,20,2,16,128]{4,3,2,1,0:T(8,128)(2,1)S(1)} %pad_maximum_fusion.3), channel_id=1, source_target_pairs={{0,2},{2,4},{4,6},{6,0},{8,10},{10,12},{12,14},{14,8},{1,3},{3,5},... | collective-permute-start | bytes 983048 | tf_op jit(solution)/shard_map/ppermute | solution.py:483
  152.1 28.2 %collective-permute-start.14 = (bf16[2,20,2,16,128]{4,3,2,1,0:T(8,128)(2,1)S(1)}, bf16[2,20,2,16,128]{4,3,2,1,0:T(8,128)(2,1)S(1)}, u32[]{:S(2)}, u32[]{:S(2)}) collective-permute-start(bf16[2,20,2,16,128]{4,3,2,1,0:T(8,128)(2,1)S(1)} %pad_maximum_fusion.2), channel_id=1, source_target_pairs={{0,4},{2,6},{4,0},{6,2},{8,12},{10,14},{12,8},{14,10},{1,5},{3,7},... | collective-permute-start | bytes 983048 | tf_op jit(solution)/shard_map/ppermute | solution.py:483
  154.1 29.2 %collective-permute-start.21 = (bf16[2,20,2,16,128]{4,3,2,1,0:T(8,128)(2,1)S(1)}, bf16[2,20,2,16,128]{4,3,2,1,0:T(8,128)(2,1)S(1)}, u32[]{:S(2)}, u32[]{:S(2)}) collective-permute-start(bf16[2,20,2,16,128]{4,3,2,1,0:T(8,128)(2,1)S(1)} %pad_maximum_fusion.4), channel_id=1, source_target_pairs={{0,6},{2,0},{4,2},{6,4},{8,14},{10,8},{12,10},{14,12},{1,7},{3,1},... | collective-permute-start | bytes 983048 | tf_op jit(solution)/shard_map/ppermute | solution.py:483
  161.3 6.5 %collective-permute-start.17 = (bf16[32,2,16,128]{3,2,1,0:T(8,128)(2,1)S(1)}, bf16[32,2,16,128]{3,2,1,0:T(8,128)(2,1)S(1)}, u32[]{:S(2)}, u32[]{:S(2)}) collective-permute-start(bf16[32,2,16,128]{3,2,1,0:T(8,128)(2,1)S(1)} %bitcast.97), channel_id=1, source_target_pairs={{0,8},{2,10},{4,12},{6,14},{8,0},{10,2},{12,4},{14,6},{1,9},{3,11}... | collective-permute-start | bytes 786440 | tf_op jit(solution)/shard_map/ppermute | solution.py:483
  183.5 3.2 %collective-permute-start.22 = (bf16[8,20,2,16,128]{4,3,2,1,0:T(8,128)(2,1)S(1)}, bf16[8,20,2,16,128]{4,3,2,1,0:T(8,128)(2,1)S(1)}, u32[]{:S(2)}, u32[]{:S(2)}) collective-permute-start(bf16[8,20,2,16,128]{4,3,2,1,0:T(8,128)(2,1)S(1)} %bitcast.86), channel_id=1, source_target_pairs={{0,1},{1,0},{2,3},{3,2},{4,5},{5,4},{6,7},{7,6},{8,9},{9,8},{10,11... | collective-permute-start | bytes 3932168 | tf_op jit(solution)/shard_map/ppermute | solution.py:483
  184.1 17.1 %collective-permute-start.18 = (bf16[2,12,2,16,128]{4,3,2,1,0:T(8,128)(2,1)S(1)}, bf16[2,12,2,16,128]{4,3,2,1,0:T(8,128)(2,1)S(1)}, u32[]{:S(2)}, u32[]{:S(2)}) collective-permute-start(bf16[2,12,2,16,128]{4,3,2,1,0:T(8,128)(2,1)S(1)} %pad_maximum_fusion.5), channel_id=1, source_target_pairs={{0,2},{2,4},{4,6},{6,0},{8,10},{10,12},{12,14},{14,8},{1,3},{3,5},... | collective-permute-start | bytes 589832 | tf_op jit(solution)/shard_map/ppermute | solution.py:483
  184.1 17.1 %collective-permute-start.19 = (bf16[2,12,2,16,128]{4,3,2,1,0:T(8,128)(2,1)S(1)}, bf16[2,12,2,16,128]{4,3,2,1,0:T(8,128)(2,1)S(1)}, u32[]{:S(2)}, u32[]{:S(2)}) collective-permute-start(bf16[2,12,2,16,128]{4,3,2,1,0:T(8,128)(2,1)S(1)} %pad_maximum_fusion.6), channel_id=1, source_target_pairs={{0,4},{2,6},{4,0},{6,2},{8,12},{10,14},{12,8},{14,10},{1,5},{3,7},... | collective-permute-start | bytes 589832 | tf_op jit(solution)/shard_map/ppermute | solution.py:483
  184.5 18.0 %collective-permute-start.20 = (bf16[2,12,2,16,128]{4,3,2,1,0:T(8,128)(2,1)S(1)}, bf16[2,12,2,16,128]{4,3,2,1,0:T(8,128)(2,1)S(1)}, u32[]{:S(2)}, u32[]{:S(2)}) collective-permute-start(bf16[2,12,2,16,128]{4,3,2,1,0:T(8,128)(2,1)S(1)} %pad_maximum_fusion.7), channel_id=1, source_target_pairs={{0,6},{2,0},{4,2},{6,4},{8,14},{10,8},{12,10},{14,12},{1,7},{3,1},... | collective-permute-start | bytes 589832 | tf_op jit(solution)/shard_map/ppermute | solution.py:483
  202.6 2.4 %collective-permute-start.23 = (bf16[8,12,2,16,128]{4,3,2,1,0:T(8,128)(2,1)S(1)}, bf16[8,12,2,16,128]{4,3,2,1,0:T(8,128)(2,1)S(1)}, u32[]{:S(2)}, u32[]{:S(2)}) collective-permute-start(bf16[8,12,2,16,128]{4,3,2,1,0:T(8,128)(2,1)S(1)} %bitcast.88), channel_id=1, source_target_pairs={{0,1},{1,0},{2,3},{3,2},{4,5},{5,4},{6,7},{7,6},{8,9},{9,8},{10,11... | collective-permute-start | bytes 2359304 | tf_op jit(solution)/shard_map/ppermute | solution.py:483
  (8 other events, 200.0 us)
